TPU v7x, 256 devices: a whole 4x4x8 slice. The times are simulated.
256 devices in a mesh: dp: 8 (over x, core), ctx: 32 (over y, z).
Axes of the slice: x: 4, y: 4, z: 8, core: 2. Of those that a mesh axis runs over, the one named last changes fastest.
Arguments:
- query_raw: bfloat16 [8, 8192, 128], P('dp', 'ctx'), may hold values from -6 to 6
- key_raw: bfloat16 [8, 8192, 128], P('dp', 'ctx'), may hold values from -6 to 6
- value_raw: bfloat16 [8, 8192, 1024], P('dp', 'ctx'), may hold values from -8 to 8
- conv_query: float32 [3, 128], replicated, may hold values from -2.5 to 2.5
- conv_key: float32 [3, 128], replicated, may hold values from -2.5 to 2.5
- conv_value: float32 [3, 1024], replicated, may hold values from -2.5 to 2.5
- norm_gain: float32 [1024], replicated, may hold values from 0.25 to 1.75
- doc_lengths: int32 [8, 8], P('dp'), may hold values from 1 to 4096, 8192 in all within a row
- out_grad: bfloat16 [8, 8192, 1024], P('dp', 'ctx'), may hold values from -6 to 6
Outputs:
- mixed: bfloat16 [8, 8192, 1024], P('dp', 'ctx')
- grad_query: bfloat16 [8, 8192, 128], P('dp', 'ctx')
- grad_key: bfloat16 [8, 8192, 128], P('dp', 'ctx')
- grad_value: bfloat16 [8, 8192, 1024], P('dp', 'ctx')
- grad_conv_query: float32 [3, 128], replicated
- grad_conv_key: float32 [3, 128], replicated
- grad_conv_value: float32 [3, 1024], replicated
- grad_gain: float32 [1024], replicated
Inputs may be any that keep to these rules, and one draw needn't show every extreme that they name: `doc_lengths`: each row holds the lengths of the 8 documents of one sequence in order; they sum to 8192 and the longest is exactly 4096.
All inputs are finite; a program needn't handle non-finite values.
Results may differ from a plain program's by a relative error of at most 0.013.
The roundings to bfloat16 on the way count: a program that leaves them out, or rounds other values in their place, can miss the bound.
Values may be sent and summed in bfloat16 or wider, within the bound.
A program may use at most 128 MiB of HBM per device.

v0:
```python
import jax
import jax.numpy as jnp
import numpy as np
from jax import lax
from jax.sharding import PartitionSpec as P

HEADS = 8
F = 16
HD = 128


norm_eps = 1e-06


def from_behind(value, axis, steps):
    count = lax.axis_size(axis)
    initial, last = (max(0, -steps), min(count, count - steps))
    return lax.ppermute(value, axis, [(source, source + steps) for source in range(initial, last)])


def entering(value, axis, join, neutral):
    count = lax.axis_size(axis)
    place = lax.axis_index(axis)
    ahead = count - 1 - place
    gathered = jax.tree.map(
        lambda a, kind: lax.all_gather(a.astype(kind), axis), value, (jnp.bfloat16, jnp.bfloat16)
    )
    state = jax.tree.map(lambda a, e: jnp.zeros_like(a) + jnp.asarray(e, a.dtype), value, neutral)

    def one(turn, state):
        source = count - 1 - turn
        return join(
            state,
            jax.tree.map(
                lambda a, own: lax.dynamic_index_in_dim(a, source, 0, False).astype(own.dtype),
                gathered,
                value,
            ),
        )

    return lax.fori_loop(0, ahead, one, state)


def features(units):
    upper_rows, upper_cols = np.triu_indices(F)
    weight = np.where(upper_rows == upper_cols, 0.5**0.5, 1.0).astype(np.float32)
    pairs = units[..., upper_rows] * units[..., upper_cols] * weight
    leading = jnp.ones(units.shape[:-1] + (1,), units.dtype)
    return jnp.concatenate([leading, units, pairs], axis=-1)


def scaled_features(units):
    return features(units * 0.5)


def state_product(form, left, right):
    return jnp.einsum(form, left, right, preferred_element_type=jnp.float32)


def doc_index(lengths, positions):
    starts = jnp.cumsum(lengths) - lengths
    hits = (positions[:, None] >= starts[None, :]).astype(jnp.int32)
    return jnp.sum(hits, axis=1) - 1


def block_mask(docs):
    order = jnp.arange(docs.shape[0], dtype=jnp.int32)
    return (order[None, :] <= order[:, None]) & (docs[None, :] == docs[:, None])


def head_kernel(query_head, key_head, mask):
    scores = jnp.dot(query_head, key_head.T, preferred_element_type=jnp.float32) * 0.25
    kernel = jnp.where(mask, 1.0 + scores + 0.5 * scores * scores, 0.0).astype(jnp.bfloat16)
    return (kernel, scores)


def conv_forward(padded, weights, tokens):
    total = (
        weights[0] * padded[2:] + weights[1] * padded[1 : tokens + 1] + weights[2] * padded[:tokens]
    )
    return total.astype(jnp.bfloat16)


def conv_backward(grads_padded, padded, weights, tokens):
    inner = grads_padded[:tokens]
    grad_signal = (
        weights[0] * grads_padded[:tokens]
        + weights[1] * grads_padded[1 : tokens + 1]
        + weights[2] * grads_padded[2:]
    )
    grad_weights = jnp.stack(
        [
            jnp.sum(inner * padded[2:], axis=0),
            jnp.sum(inner * padded[1 : tokens + 1], axis=0),
            jnp.sum(inner * padded[:tokens], axis=0),
        ]
    )
    return (grad_signal.astype(jnp.bfloat16), grad_weights)


def tail_state(key_conv, value_conv, use_next):
    tokens = key_conv.shape[0]
    phi_key = scaled_features(key_conv.reshape(tokens, HEADS, F).astype(jnp.float32)).astype(
        jnp.bfloat16
    )
    masked = phi_key * use_next.astype(jnp.bfloat16)[:, None, None]
    return state_product("thf,thd->hfd", masked, value_conv.reshape(tokens, HEADS, HD))


def forward_block(
    query_conv, key_conv, value_conv, docs, use_prev, incoming, upstream_raw, norm_gain
):
    tokens = query_conv.shape[0]
    mask = block_mask(docs)
    query_heads = jnp.moveaxis(query_conv.reshape(tokens, HEADS, F), 1, 0)
    key_heads = jnp.moveaxis(key_conv.reshape(tokens, HEADS, F), 1, 0)
    value_heads = jnp.moveaxis(value_conv.reshape(tokens, HEADS, HD), 1, 0)

    def forward_per_head(pieces):
        kernel, scores = head_kernel(pieces[0], pieces[1], mask)
        inner = jnp.dot(kernel, pieces[2], preferred_element_type=jnp.float32)
        return (kernel, scores, inner)

    kernels, scores, inner = lax.map(forward_per_head, (query_heads, key_heads, value_heads))
    phi_query = scaled_features(query_conv.reshape(tokens, HEADS, F).astype(jnp.float32)).astype(
        jnp.bfloat16
    )
    prev_mask = use_prev[:, None, None]
    cross = state_product("thf,hfd->thd", phi_query, incoming.astype(jnp.bfloat16))
    attended = jnp.moveaxis(inner, 0, 1) + cross * prev_mask
    scale = jnp.sqrt(jnp.mean(attended * attended, axis=-1, keepdims=True) + norm_eps)
    normed = attended / scale
    gains = norm_gain.reshape(HEADS, HD)
    mixed = (normed * gains).reshape(tokens, HEADS * HD).astype(jnp.bfloat16)
    upstream = upstream_raw.reshape(tokens, HEADS, HD).astype(jnp.float32)
    gain_part = jnp.sum(upstream * normed, axis=0).reshape(HEADS * HD)
    pulled = upstream * gains
    grad_attended = (
        (pulled - normed * jnp.mean(pulled * normed, axis=-1, keepdims=True)) / scale
    ).astype(jnp.bfloat16)
    masked_query = phi_query * use_prev.astype(jnp.bfloat16)[:, None, None]
    head_state = state_product("thf,thd->hfd", masked_query, grad_attended)
    return (mixed, grad_attended, gain_part, head_state, kernels, scores)


def backward_block(
    query_conv,
    key_conv,
    value_conv,
    docs,
    use_prev,
    use_next,
    incoming,
    outgoing,
    grad_attended,
    kernels,
    scores,
):
    tokens = query_conv.shape[0]
    mask = block_mask(docs)
    query_heads = jnp.moveaxis(query_conv.reshape(tokens, HEADS, F), 1, 0)
    key_heads = jnp.moveaxis(key_conv.reshape(tokens, HEADS, F), 1, 0)
    value_heads = jnp.moveaxis(value_conv.reshape(tokens, HEADS, HD), 1, 0)
    grad_heads = jnp.moveaxis(grad_attended.reshape(tokens, HEADS, HD), 1, 0)

    def backward_per_head(pieces):
        query_head, key_head, value_head, grad_head, kernel, score = pieces
        grad_kernel = jnp.dot(grad_head, value_head.T, preferred_element_type=jnp.float32)
        grad_scores = jnp.where(mask, grad_kernel * (1.0 + score), 0.0).astype(jnp.bfloat16)
        grad_query = jnp.dot(grad_scores, key_head, preferred_element_type=jnp.float32) * 0.25
        grad_key = jnp.dot(grad_scores.T, query_head, preferred_element_type=jnp.float32) * 0.25
        grad_value = jnp.dot(kernel.T, grad_head, preferred_element_type=jnp.float32)
        return (grad_query, grad_key, grad_value)

    inner_query, inner_key, inner_value = lax.map(
        backward_per_head, (query_heads, key_heads, value_heads, grad_heads, kernels, scores)
    )
    query_units = query_conv.reshape(tokens, HEADS, F).astype(jnp.float32)
    key_units = key_conv.reshape(tokens, HEADS, F).astype(jnp.float32)
    values = value_conv.reshape(tokens, HEADS, HD)
    upstream = grad_attended.reshape(tokens, HEADS, HD)
    incoming_low = incoming.astype(jnp.bfloat16)
    outgoing_low = outgoing.astype(jnp.bfloat16)
    prev_mask = use_prev[:, None, None]
    next_mask = use_next[:, None, None]
    phi_query, pull_query = jax.vjp(scaled_features, query_units)
    phi_key, pull_key = jax.vjp(scaled_features, key_units)
    grad_phi_query = state_product("thd,hfd->thf", upstream, incoming_low) * prev_mask
    grad_phi_key = state_product("thd,hfd->thf", values, outgoing_low) * next_mask
    cross_value = (
        state_product("thf,hfd->thd", phi_key.astype(jnp.bfloat16), outgoing_low) * next_mask
    )
    total_query = jnp.moveaxis(inner_query, 0, 1) + pull_query(grad_phi_query)[0]
    total_key = jnp.moveaxis(inner_key, 0, 1) + pull_key(grad_phi_key)[0]
    total_value = jnp.moveaxis(inner_value, 0, 1) + cross_value
    return (
        total_query.reshape(tokens, HEADS * F),
        total_key.reshape(tokens, HEADS * F),
        total_value.reshape(tokens, HEADS * HD),
    )


def combine_states(earlier, later):
    return (later[0] + (1.0 - later[1]) * earlier[0], jnp.maximum(earlier[1], later[1]))


def shards(
    query_raw,
    key_raw,
    value_raw,
    conv_query,
    conv_key,
    conv_value,
    norm_gain,
    doc_lengths,
    out_grad,
):
    tokens = query_raw.shape[1]
    width = query_raw.shape[2]
    rims = jnp.concatenate(
        [query_raw[0, tokens - 2 :], key_raw[0, tokens - 2 :], value_raw[0, tokens - 2 :]], axis=1
    )
    before = from_behind(rims, "ctx", 1)
    query_padded = jnp.concatenate([before[:, :width], query_raw[0]], axis=0).astype(jnp.float32)
    key_padded = jnp.concatenate([before[:, width : 2 * width], key_raw[0]], axis=0).astype(
        jnp.float32
    )
    value_padded = jnp.concatenate([before[:, 2 * width :], value_raw[0]], axis=0).astype(
        jnp.float32
    )
    query_conv = conv_forward(query_padded, conv_query, tokens)
    key_conv = conv_forward(key_padded, conv_key, tokens)
    value_conv = conv_forward(value_padded, conv_value, tokens)
    first_position = lax.axis_index("ctx") * tokens
    positions = first_position + jnp.arange(tokens, dtype=jnp.int32)
    lengths = doc_lengths[0]
    docs = doc_index(lengths, positions)
    edges = doc_index(lengths, jnp.stack([first_position - 1, first_position + tokens - 1]))
    use_prev = (docs == edges[0]).astype(jnp.float32)
    use_next = (docs == edges[1]).astype(jnp.float32)
    reset = (edges[0] != edges[1]).astype(jnp.float32)
    tail = tail_state(key_conv, value_conv, use_next)
    zero_state = jnp.zeros_like(tail)
    zero_flag = jnp.zeros((), jnp.float32)

    def relay_step(step, carry):
        received = from_behind(carry[1], "ctx", 1)
        return (received, tail + (1.0 - reset) * received)

    incoming, reached = lax.fori_loop(0, lax.axis_size("ctx"), relay_step, (zero_state, tail))
    mixed, grad_attended, gain_part, head_state, kernels, scores = forward_block(
        query_conv, key_conv, value_conv, docs, use_prev, incoming, out_grad[0], norm_gain
    )
    outgoing, passed = entering((head_state, reset), "ctx", combine_states, (zero_state, zero_flag))
    grad_q_conv, grad_k_conv, grad_v_conv = backward_block(
        query_conv,
        key_conv,
        value_conv,
        docs,
        use_prev,
        use_next,
        incoming,
        outgoing,
        grad_attended,
        kernels,
        scores,
    )
    leading_rows = jnp.concatenate([grad_q_conv[:2], grad_k_conv[:2], grad_v_conv[:2]], axis=1)
    after = from_behind(leading_rows, "ctx", -1)
    grad_query, conv_grad_query = conv_backward(
        jnp.concatenate([grad_q_conv, after[:, :width]], axis=0), query_padded, conv_query, tokens
    )
    grad_key, conv_grad_key = conv_backward(
        jnp.concatenate([grad_k_conv, after[:, width : 2 * width]], axis=0),
        key_padded,
        conv_key,
        tokens,
    )
    grad_value, conv_grad_value = conv_backward(
        jnp.concatenate([grad_v_conv, after[:, 2 * width :]], axis=0),
        value_padded,
        conv_value,
        tokens,
    )
    totals = lax.psum((conv_grad_query, conv_grad_key, conv_grad_value, gain_part), ("dp", "ctx"))
    return (
        mixed[None],
        grad_query[None],
        grad_key[None],
        grad_value[None],
        totals[0],
        totals[1],
        totals[2],
        totals[3],
    )


def solution(mesh):
    placed = (
        P("dp", "ctx", None),
        P("dp", "ctx", None),
        P("dp", "ctx", None),
        P(),
        P(),
        P(),
        P(),
        P("dp", None),
        P("dp", "ctx", None),
    )
    return jax.shard_map(
        shards,
        mesh=mesh,
        in_specs=placed,
        out_specs=(
            P("dp", "ctx", None),
            P("dp", "ctx", None),
            P("dp", "ctx", None),
            P("dp", "ctx", None),
            P(),
            P(),
            P(),
            P(),
        ),
        check_vma=False,
    )
```

profile of v0, /device:TPU:1, one launch (start us, length us, event | category | flops | bytes accessed | tf_op | source)
XLA Modules:
  0.0 998.8 jit_solution(12797186317861324070)
XLA Ops:
  43.5 532.7 %while.60 = (s32[]{:T(128)}, f32[8,153,128]{2,0,1:T(8,128)}, f32[8,153,128]{2,0,1:T(8,128)}, f32[]{:T(128)}, f32[8,153,128]{2,0,1:T(8,128)S(1)}, /*index=5*/s32[]{:T(128)}) while((s32[]{:T(128)}, f32[8,153,128]{2,0,1:T(8,128)}, f32[8,153,128]{2,0,1:T(8,128)}, f32[]{:T(128)}, f32[8,153,128]{2,0,1:T(8,128)S(1)}, /*index=5*/s32[]{:T(128)}) %tuple.141), condition=%wide.region_6.7_spmd, body=%wide.region_5.6_spmd.sunk | while | flops 313346 | bytes 6893709 | solution.py:250
  47.1 12.7 %collective-permute-done = f32[8,153,128]{2,0,1:T(8,128)S(1)} collective-permute-done((f32[8,153,128]{2,0,1:T(8,128)}, f32[8,153,128]{2,0,1:T(8,128)S(1)}, u32[]{:S(2)}, u32[]{:S(2)}) %collective-permute-start) | collective-permute-done | bytes 626720 | tf_op jit(solution)/shard_map/while/body/eval_jaxpr/ppermute | solution.py:18
  64.9 11.8 %collective-permute-done = f32[8,153,128]{2,0,1:T(8,128)S(1)} collective-permute-done((f32[8,153,128]{2,0,1:T(8,128)}, f32[8,153,128]{2,0,1:T(8,128)S(1)}, u32[]{:S(2)}, u32[]{:S(2)}) %collective-permute-start) | collective-permute-done | bytes 626720 | tf_op jit(solution)/shard_map/while/body/eval_jaxpr/ppermute | solution.py:18
  82.1 10.9 %collective-permute-done = f32[8,153,128]{2,0,1:T(8,128)S(1)} collective-permute-done((f32[8,153,128]{2,0,1:T(8,128)}, f32[8,153,128]{2,0,1:T(8,128)S(1)}, u32[]{:S(2)}, u32[]{:S(2)}) %collective-permute-start) | collective-permute-done | bytes 626720 | tf_op jit(solution)/shard_map/while/body/eval_jaxpr/ppermute | solution.py:18
  98.1 10.0 collective-permute-done
  113.1 9.0 collective-permute-done
  128.3 8.1 collective-permute-done
  142.7 7.5 collective-permute-done
  156.5 7.5 collective-permute-done
  170.3 8.2 collective-permute-done
  184.8 9.0 collective-permute-done
  200.4 10.0 %collective-permute-done = f32[8,153,128]{2,0,1:T(8,128)S(1)} collective-permute-done((f32[8,153,128]{2,0,1:T(8,128)}, f32[8,153,128]{2,0,1:T(8,128)S(1)}, u32[]{:S(2)}, u32[]{:S(2)}) %collective-permute-start) | collective-permute-done | bytes 626720 | tf_op jit(solution)/shard_map/while/body/eval_jaxpr/ppermute | solution.py:18
  217.3 11.1 %collective-permute-done = f32[8,153,128]{2,0,1:T(8,128)S(1)} collective-permute-done((f32[8,153,128]{2,0,1:T(8,128)}, f32[8,153,128]{2,0,1:T(8,128)S(1)}, u32[]{:S(2)}, u32[]{:S(2)}) %collective-permute-start) | collective-permute-done | bytes 626720 | tf_op jit(solution)/shard_map/while/body/eval_jaxpr/ppermute | solution.py:18
  235.3 12.2 %collective-permute-done = f32[8,153,128]{2,0,1:T(8,128)S(1)} collective-permute-done((f32[8,153,128]{2,0,1:T(8,128)}, f32[8,153,128]{2,0,1:T(8,128)S(1)}, u32[]{:S(2)}, u32[]{:S(2)}) %collective-permute-start) | collective-permute-done | bytes 626720 | tf_op jit(solution)/shard_map/while/body/eval_jaxpr/ppermute | solution.py:18
  254.3 13.2 %collective-permute-done = f32[8,153,128]{2,0,1:T(8,128)S(1)} collective-permute-done((f32[8,153,128]{2,0,1:T(8,128)}, f32[8,153,128]{2,0,1:T(8,128)S(1)}, u32[]{:S(2)}, u32[]{:S(2)}) %collective-permute-start) | collective-permute-done | bytes 626720 | tf_op jit(solution)/shard_map/while/body/eval_jaxpr/ppermute | solution.py:18
  274.5 13.9 %collective-permute-done = f32[8,153,128]{2,0,1:T(8,128)S(1)} collective-permute-done((f32[8,153,128]{2,0,1:T(8,128)}, f32[8,153,128]{2,0,1:T(8,128)S(1)}, u32[]{:S(2)}, u32[]{:S(2)}) %collective-permute-start) | collective-permute-done | bytes 626720 | tf_op jit(solution)/shard_map/while/body/eval_jaxpr/ppermute | solution.py:18
  294.8 12.8 %collective-permute-done = f32[8,153,128]{2,0,1:T(8,128)S(1)} collective-permute-done((f32[8,153,128]{2,0,1:T(8,128)}, f32[8,153,128]{2,0,1:T(8,128)S(1)}, u32[]{:S(2)}, u32[]{:S(2)}) %collective-permute-start) | collective-permute-done | bytes 626720 | tf_op jit(solution)/shard_map/while/body/eval_jaxpr/ppermute | solution.py:18
  313.3 11.6 %collective-permute-done = f32[8,153,128]{2,0,1:T(8,128)S(1)} collective-permute-done((f32[8,153,128]{2,0,1:T(8,128)}, f32[8,153,128]{2,0,1:T(8,128)S(1)}, u32[]{:S(2)}, u32[]{:S(2)}) %collective-permute-start) | collective-permute-done | bytes 626720 | tf_op jit(solution)/shard_map/while/body/eval_jaxpr/ppermute | solution.py:18
  331.0 10.6 %collective-permute-done = f32[8,153,128]{2,0,1:T(8,128)S(1)} collective-permute-done((f32[8,153,128]{2,0,1:T(8,128)}, f32[8,153,128]{2,0,1:T(8,128)S(1)}, u32[]{:S(2)}, u32[]{:S(2)}) %collective-permute-start) | collective-permute-done | bytes 626720 | tf_op jit(solution)/shard_map/while/body/eval_jaxpr/ppermute | solution.py:18
  347.9 9.7 collective-permute-done
  363.9 8.8 collective-permute-done
  378.9 7.8 collective-permute-done
  393.0 7.5 collective-permute-done
  406.8 7.6 collective-permute-done
  415.5 7.8 collective-permute-start
  423.3 7.5 collective-permute-done
  431.9 6.1 collective-permute-start
  438.0 7.6 collective-permute-done
  452.8 8.4 collective-permute-done
  462.2 6.1 collective-permute-start
  468.4 9.2 collective-permute-done
  478.6 6.1 collective-permute-start
  484.7 9.9 collective-permute-done
  501.9 10.7 %collective-permute-done = f32[8,153,128]{2,0,1:T(8,128)S(1)} collective-permute-done((f32[8,153,128]{2,0,1:T(8,128)}, f32[8,153,128]{2,0,1:T(8,128)S(1)}, u32[]{:S(2)}, u32[]{:S(2)}) %collective-permute-start) | collective-permute-done | bytes 626720 | tf_op jit(solution)/shard_map/while/body/eval_jaxpr/ppermute | solution.py:18
  519.8 11.5 %collective-permute-done = f32[8,153,128]{2,0,1:T(8,128)S(1)} collective-permute-done((f32[8,153,128]{2,0,1:T(8,128)}, f32[8,153,128]{2,0,1:T(8,128)S(1)}, u32[]{:S(2)}, u32[]{:S(2)}) %collective-permute-start) | collective-permute-done | bytes 626720 | tf_op jit(solution)/shard_map/while/body/eval_jaxpr/ppermute | solution.py:18
  532.4 7.6 collective-permute-start
  540.0 12.6 %collective-permute-done = f32[8,153,128]{2,0,1:T(8,128)S(1)} collective-permute-done((f32[8,153,128]{2,0,1:T(8,128)}, f32[8,153,128]{2,0,1:T(8,128)S(1)}, u32[]{:S(2)}, u32[]{:S(2)}) %collective-permute-start) | collective-permute-done | bytes 626720 | tf_op jit(solution)/shard_map/while/body/eval_jaxpr/ppermute | solution.py:18
  553.6 7.9 collective-permute-start
  561.5 13.7 %collective-permute-done = f32[8,153,128]{2,0,1:T(8,128)S(1)} collective-permute-done((f32[8,153,128]{2,0,1:T(8,128)}, f32[8,153,128]{2,0,1:T(8,128)S(1)}, u32[]{:S(2)}, u32[]{:S(2)}) %collective-permute-start) | collective-permute-done | bytes 626720 | tf_op jit(solution)/shard_map/while/body/eval_jaxpr/ppermute | solution.py:18
  578.2 27.4 %while.62 = (s32[]{:T(128)}, bf16[8,256,256]{2,1,0:T(8,128)(2,1)}, f32[8,256,256]{2,1,0:T(8,128)}, f32[8,256,128]{1,2,0:T(8,128)S(1)}, bf16[8,256,16]{1,2,0:T(8,...) while((s32[]{:T(128)}, bf16[8,256,256]{2,1,0:T(8,128)(2,1)}, ...), condition=%wide.region_3.4_spmd.clone, body=%wide.region_2.3_spmd.clone.sunk | while | flops 20250624 | bytes 1399401 | solution.py:124
  611.9 77.9 %all-reduce = bf16[32]{0:T(256)(128)(2,1)} all-reduce(bf16[32]{0:T(256)(128)(2,1)S(1)} %dynamic-update-slice), channel_id=1, replica_groups=mesh['dp'=8,'ctx'=32] {'ctx'}, use_global_device_ids=true, to_apply=%add | all-reduce | flops 32 | bytes 128
  691.5 36.9 %while.63 = (s32[]{:T(128)}, f32[8,256,16]{1,2,0:T(8,128)}, f32[8,256,16]{1,2,0:T(8,128)}, f32[8,256,128]{1,2,0:T(8,128)S(1)}, bf16[8,256,128]{1,2,0:T(8,128)(2,...) while((s32[]{:T(128)}, f32[8,256,16]{1,2,0:T(8,128)}, ...), condition=%wide.region_10.11_spmd.clone, body=%wide.region_9.10_spmd.clone.sunk | while | flops 38215680 | bytes 1170557 | solution.py:175
  728.5 50.4 %all-gather.3.cloned.1.call-done = bf16[256,153,128]{2,0,1:T(8,128)(2,1)} async-done(((bf16[8,153,128]{2,0,1:T(8,128)(2,1)}), bf16[256,153,128]{2,0,1:T(8,128)(2,1)}) %all-gather.3.cloned.1.call-update) | async-done | bytes 10027024 | tf_op jit(solution)/shard_map/all_gather | solution.py:26
  778.9 77.0 %while.61 = (s32[]{:T(128)}, f32[8,153,128]{2,1,0:T(8,128)S(1)}, s32[]{:T(128)}, bf16[32,8,153,128]{3,1,0,2:T(8,128)(2,1)}, bf16[32]{0:T(256)(128)(2,1)S(1)}, /*...) while((s32[]{:T(128)}, f32[8,153,128]{2,1,0:T(8,128)S(1)}, s32[]{:T(128)}, ...), condition=%wide.region_14.15_spmd, body=%wide.region_13.14_spmd.sunk | while | flops 470023 | bytes 2193589 | solution.py:41
  867.0 11.8 %scatter_fusion = f32[256,8,16]{0,1,2:T(8,128)S(1)} fusion(f32[256,8,16]{0,1,2:T(8,128)S(1)} %copy.201, s32[136]{0:T(256)S(1)} %copy-done.40, f32[136,256,8]{1,2,0:T(8,128)} %copy.202), kind=kCustom, calls=%fused_computation.4 | custom fusion | flops 278528 | bytes 3342880 | tf_op jit(solution)/shard_map/transpose(jvp())/scatter-add | solution.py:47
  878.8 6.1 scatter_fusion.1
  888.2 12.0 %scatter_fusion.3 = f32[256,8,16]{0,1,2:T(8,128)S(1)} fusion(f32[256,8,16]{0,1,2:T(8,128)S(1)} %broadcast.134.clone.1, s32[136]{0:T(256)S(1)} %copy-done.41, f32[136,256,8]{1,2,0:T(8,128)} %copy.213), kind=kCustom, calls=%fused_computation.7 | custom fusion | flops 278528 | bytes 3342880 | tf_op jit(solution)/shard_map/transpose(jvp())/scatter-add | solution.py:47
  914.5 77.5 %all-reduce.1 = (f32[3,128]{1,0:T(4,128)}, f32[3,128]{1,0:T(4,128)}, f32[3,1024]{1,0:T(4,128)}, f32[1024]{0:T(1024)}) all-reduce(f32[3,128]{1,0:T(4,128)S(1)} %pad_maximum_fusion.12, f32[3,128]{1,0:T(4,128)S(1)} %pad_maximum_fusion.13, f32[3,1024]{1,0:T(4,128)S(1)} %pad_maximum_fusion.9, ...), channel_id=1, replica_groups=mesh['dp'=8,'ctx'=32] {'dp','ctx'}, use_global_device_ids=true, to_apply=%region_20.21 | all-reduce | flops 4864 | bytes 38912 | tf_op jit(solution)/shard_map/psum | solution.py:285
  (485 shorter events, 360.5 us)
Async XLA Ops:
  7.2 18.7 %copy-start.30 = (bf16[1,256,1024]{2,1,0:T(8,128)(2,1)S(1)}, bf16[1,256,1024]{2,1,0:T(8,128)(2,1)}, u32[]{:S(2)}) copy-start(bf16[1,256,1024]{2,1,0:T(8,128)(2,1)} %param.39) | copy-start | bytes 1572868
  7.2 771.6 %all-gather.3.cloned.1.call-start = ((), (), s32[]{:S(2)}) async-start(), calls=%async_computation | async-start | bytes 10340352 | tf_op jit(solution)/shard_map/all_gather | solution.py:26
  8.7 17.2 %collective-permute-start.1 = (bf16[2,1280]{1,0:T(2,128)(2,1)S(1)}, bf16[2,1280]{1,0:T(2,128)(2,1)S(1)}, u32[]{:S(2)}, u32[]{:S(2)}) collective-permute-start(bf16[2,1280]{1,0:T(2,128)(2,1)S(1)} %pad_maximum_fusion.11), channel_id=1, source_target_pairs={{0,1},{1,2},{2,3},{3,4},{4,5},{5,6},{6,7},{7,8},{8,9},{9,10},{10,1... | collective-permute-start | bytes 15368 | tf_op jit(solution)/shard_map/ppermute | solution.py:18
  16.9 12.3 %copy-start.42 = (f32[128]{0:T(128)}, f32[128]{0:T(128)S(1)}, u32[]{:S(2)}) copy-start(f32[128]{0:T(128)S(1)} %get-tuple-element.563) | copy-start | bytes 1540
  16.9 12.4 %copy-start.44 = (f32[128]{0:T(128)}, f32[128]{0:T(128)S(1)}, u32[]{:S(2)}) copy-start(f32[128]{0:T(128)S(1)} %get-tuple-element.564) | copy-start | bytes 1540
  43.5 16.3 %collective-permute-start = (f32[8,153,128]{2,0,1:T(8,128)}, f32[8,153,128]{2,0,1:T(8,128)S(1)}, u32[]{:S(2)}, u32[]{:S(2)}) collective-permute-start(f32[8,153,128]{2,0,1:T(8,128)} %get-tuple-element.766), channel_id=1, source_target_pairs={{0,1},{1,2},{2,3},{3,4},{4,5},{5,6},{6,7},{7,8},{8,9},{9,10},{10,1... | collective-permute-start | bytes 1880072 | tf_op jit(solution)/shard_map/while/body/eval_jaxpr/ppermute | solution.py:18
  60.9 15.8 %collective-permute-start = (f32[8,153,128]{2,0,1:T(8,128)}, f32[8,153,128]{2,0,1:T(8,128)S(1)}, u32[]{:S(2)}, u32[]{:S(2)}) collective-permute-start(f32[8,153,128]{2,0,1:T(8,128)} %get-tuple-element.766), channel_id=1, source_target_pairs={{0,1},{1,2},{2,3},{3,4},{4,5},{5,6},{6,7},{7,8},{8,9},{9,10},{10,1... | collective-permute-start | bytes 1880072 | tf_op jit(solution)/shard_map/while/body/eval_jaxpr/ppermute | solution.py:18
  77.8 15.2 %collective-permute-start = (f32[8,153,128]{2,0,1:T(8,128)}, f32[8,153,128]{2,0,1:T(8,128)S(1)}, u32[]{:S(2)}, u32[]{:S(2)}) collective-permute-start(f32[8,153,128]{2,0,1:T(8,128)} %get-tuple-element.766), channel_id=1, source_target_pairs={{0,1},{1,2},{2,3},{3,4},{4,5},{5,6},{6,7},{7,8},{8,9},{9,10},{10,1... | collective-permute-start | bytes 1880072 | tf_op jit(solution)/shard_map/while/body/eval_jaxpr/ppermute | solution.py:18
  94.0 14.0 %collective-permute-start = (f32[8,153,128]{2,0,1:T(8,128)}, f32[8,153,128]{2,0,1:T(8,128)S(1)}, u32[]{:S(2)}, u32[]{:S(2)}) collective-permute-start(f32[8,153,128]{2,0,1:T(8,128)} %get-tuple-element.766), channel_id=1, source_target_pairs={{0,1},{1,2},{2,3},{3,4},{4,5},{5,6},{6,7},{7,8},{8,9},{9,10},{10,1... | collective-permute-start | bytes 1880072 | tf_op jit(solution)/shard_map/while/body/eval_jaxpr/ppermute | solution.py:18
  109.1 13.1 %collective-permute-start = (f32[8,153,128]{2,0,1:T(8,128)}, f32[8,153,128]{2,0,1:T(8,128)S(1)}, u32[]{:S(2)}, u32[]{:S(2)}) collective-permute-start(f32[8,153,128]{2,0,1:T(8,128)} %get-tuple-element.766), channel_id=1, source_target_pairs={{0,1},{1,2},{2,3},{3,4},{4,5},{5,6},{6,7},{7,8},{8,9},{9,10},{10,1... | collective-permute-start | bytes 1880072 | tf_op jit(solution)/shard_map/while/body/eval_jaxpr/ppermute | solution.py:18
  123.2 13.2 %collective-permute-start = (f32[8,153,128]{2,0,1:T(8,128)}, f32[8,153,128]{2,0,1:T(8,128)S(1)}, u32[]{:S(2)}, u32[]{:S(2)}) collective-permute-start(f32[8,153,128]{2,0,1:T(8,128)} %get-tuple-element.766), channel_id=1, source_target_pairs={{0,1},{1,2},{2,3},{3,4},{4,5},{5,6},{6,7},{7,8},{8,9},{9,10},{10,1... | collective-permute-start | bytes 1880072 | tf_op jit(solution)/shard_map/while/body/eval_jaxpr/ppermute | solution.py:18
  137.5 12.7 %collective-permute-start = (f32[8,153,128]{2,0,1:T(8,128)}, f32[8,153,128]{2,0,1:T(8,128)S(1)}, u32[]{:S(2)}, u32[]{:S(2)}) collective-permute-start(f32[8,153,128]{2,0,1:T(8,128)} %get-tuple-element.766), channel_id=1, source_target_pairs={{0,1},{1,2},{2,3},{3,4},{4,5},{5,6},{6,7},{7,8},{8,9},{9,10},{10,1... | collective-permute-start | bytes 1880072 | tf_op jit(solution)/shard_map/while/body/eval_jaxpr/ppermute | solution.py:18
  151.3 12.7 %collective-permute-start = (f32[8,153,128]{2,0,1:T(8,128)}, f32[8,153,128]{2,0,1:T(8,128)S(1)}, u32[]{:S(2)}, u32[]{:S(2)}) collective-permute-start(f32[8,153,128]{2,0,1:T(8,128)} %get-tuple-element.766), channel_id=1, source_target_pairs={{0,1},{1,2},{2,3},{3,4},{4,5},{5,6},{6,7},{7,8},{8,9},{9,10},{10,1... | collective-permute-start | bytes 1880072 | tf_op jit(solution)/shard_map/while/body/eval_jaxpr/ppermute | solution.py:18
  165.0 13.4 %collective-permute-start = (f32[8,153,128]{2,0,1:T(8,128)}, f32[8,153,128]{2,0,1:T(8,128)S(1)}, u32[]{:S(2)}, u32[]{:S(2)}) collective-permute-start(f32[8,153,128]{2,0,1:T(8,128)} %get-tuple-element.766), channel_id=1, source_target_pairs={{0,1},{1,2},{2,3},{3,4},{4,5},{5,6},{6,7},{7,8},{8,9},{9,10},{10,1... | collective-permute-start | bytes 1880072 | tf_op jit(solution)/shard_map/while/body/eval_jaxpr/ppermute | solution.py:18
  179.5 14.2 %collective-permute-start = (f32[8,153,128]{2,0,1:T(8,128)}, f32[8,153,128]{2,0,1:T(8,128)S(1)}, u32[]{:S(2)}, u32[]{:S(2)}) collective-permute-start(f32[8,153,128]{2,0,1:T(8,128)} %get-tuple-element.766), channel_id=1, source_target_pairs={{0,1},{1,2},{2,3},{3,4},{4,5},{5,6},{6,7},{7,8},{8,9},{9,10},{10,1... | collective-permute-start | bytes 1880072 | tf_op jit(solution)/shard_map/while/body/eval_jaxpr/ppermute | solution.py:18
  194.8 15.6 %collective-permute-start = (f32[8,153,128]{2,0,1:T(8,128)}, f32[8,153,128]{2,0,1:T(8,128)S(1)}, u32[]{:S(2)}, u32[]{:S(2)}) collective-permute-start(f32[8,153,128]{2,0,1:T(8,128)} %get-tuple-element.766), channel_id=1, source_target_pairs={{0,1},{1,2},{2,3},{3,4},{4,5},{5,6},{6,7},{7,8},{8,9},{9,10},{10,1... | collective-permute-start | bytes 1880072 | tf_op jit(solution)/shard_map/while/body/eval_jaxpr/ppermute | solution.py:18
  211.4 16.9 %collective-permute-start = (f32[8,153,128]{2,0,1:T(8,128)}, f32[8,153,128]{2,0,1:T(8,128)S(1)}, u32[]{:S(2)}, u32[]{:S(2)}) collective-permute-start(f32[8,153,128]{2,0,1:T(8,128)} %get-tuple-element.766), channel_id=1, source_target_pairs={{0,1},{1,2},{2,3},{3,4},{4,5},{5,6},{6,7},{7,8},{8,9},{9,10},{10,1... | collective-permute-start | bytes 1880072 | tf_op jit(solution)/shard_map/while/body/eval_jaxpr/ppermute | solution.py:18
  229.4 18.0 %collective-permute-start = (f32[8,153,128]{2,0,1:T(8,128)}, f32[8,153,128]{2,0,1:T(8,128)S(1)}, u32[]{:S(2)}, u32[]{:S(2)}) collective-permute-start(f32[8,153,128]{2,0,1:T(8,128)} %get-tuple-element.766), channel_id=1, source_target_pairs={{0,1},{1,2},{2,3},{3,4},{4,5},{5,6},{6,7},{7,8},{8,9},{9,10},{10,1... | collective-permute-start | bytes 1880072 | tf_op jit(solution)/shard_map/while/body/eval_jaxpr/ppermute | solution.py:18
  248.5 19.1 %collective-permute-start = (f32[8,153,128]{2,0,1:T(8,128)}, f32[8,153,128]{2,0,1:T(8,128)S(1)}, u32[]{:S(2)}, u32[]{:S(2)}) collective-permute-start(f32[8,153,128]{2,0,1:T(8,128)} %get-tuple-element.766), channel_id=1, source_target_pairs={{0,1},{1,2},{2,3},{3,4},{4,5},{5,6},{6,7},{7,8},{8,9},{9,10},{10,1... | collective-permute-start | bytes 1880072 | tf_op jit(solution)/shard_map/while/body/eval_jaxpr/ppermute | solution.py:18
  268.6 19.8 %collective-permute-start = (f32[8,153,128]{2,0,1:T(8,128)}, f32[8,153,128]{2,0,1:T(8,128)S(1)}, u32[]{:S(2)}, u32[]{:S(2)}) collective-permute-start(f32[8,153,128]{2,0,1:T(8,128)} %get-tuple-element.766), channel_id=1, source_target_pairs={{0,1},{1,2},{2,3},{3,4},{4,5},{5,6},{6,7},{7,8},{8,9},{9,10},{10,1... | collective-permute-start | bytes 1880072 | tf_op jit(solution)/shard_map/while/body/eval_jaxpr/ppermute | solution.py:18
  289.4 18.2 %collective-permute-start = (f32[8,153,128]{2,0,1:T(8,128)}, f32[8,153,128]{2,0,1:T(8,128)S(1)}, u32[]{:S(2)}, u32[]{:S(2)}) collective-permute-start(f32[8,153,128]{2,0,1:T(8,128)} %get-tuple-element.766), channel_id=1, source_target_pairs={{0,1},{1,2},{2,3},{3,4},{4,5},{5,6},{6,7},{7,8},{8,9},{9,10},{10,1... | collective-permute-start | bytes 1880072 | tf_op jit(solution)/shard_map/while/body/eval_jaxpr/ppermute | solution.py:18
  308.7 16.1 %collective-permute-start = (f32[8,153,128]{2,0,1:T(8,128)}, f32[8,153,128]{2,0,1:T(8,128)S(1)}, u32[]{:S(2)}, u32[]{:S(2)}) collective-permute-start(f32[8,153,128]{2,0,1:T(8,128)} %get-tuple-element.766), channel_id=1, source_target_pairs={{0,1},{1,2},{2,3},{3,4},{4,5},{5,6},{6,7},{7,8},{8,9},{9,10},{10,1... | collective-permute-start | bytes 1880072 | tf_op jit(solution)/shard_map/while/body/eval_jaxpr/ppermute | solution.py:18
  325.9 15.7 %collective-permute-start = (f32[8,153,128]{2,0,1:T(8,128)}, f32[8,153,128]{2,0,1:T(8,128)S(1)}, u32[]{:S(2)}, u32[]{:S(2)}) collective-permute-start(f32[8,153,128]{2,0,1:T(8,128)} %get-tuple-element.766), channel_id=1, source_target_pairs={{0,1},{1,2},{2,3},{3,4},{4,5},{5,6},{6,7},{7,8},{8,9},{9,10},{10,1... | collective-permute-start | bytes 1880072 | tf_op jit(solution)/shard_map/while/body/eval_jaxpr/ppermute | solution.py:18
  342.6 14.9 %collective-permute-start = (f32[8,153,128]{2,0,1:T(8,128)}, f32[8,153,128]{2,0,1:T(8,128)S(1)}, u32[]{:S(2)}, u32[]{:S(2)}) collective-permute-start(f32[8,153,128]{2,0,1:T(8,128)} %get-tuple-element.766), channel_id=1, source_target_pairs={{0,1},{1,2},{2,3},{3,4},{4,5},{5,6},{6,7},{7,8},{8,9},{9,10},{10,1... | collective-permute-start | bytes 1880072 | tf_op jit(solution)/shard_map/while/body/eval_jaxpr/ppermute | solution.py:18
  358.6 14.0 %collective-permute-start = (f32[8,153,128]{2,0,1:T(8,128)}, f32[8,153,128]{2,0,1:T(8,128)S(1)}, u32[]{:S(2)}, u32[]{:S(2)}) collective-permute-start(f32[8,153,128]{2,0,1:T(8,128)} %get-tuple-element.766), channel_id=1, source_target_pairs={{0,1},{1,2},{2,3},{3,4},{4,5},{5,6},{6,7},{7,8},{8,9},{9,10},{10,1... | collective-permute-start | bytes 1880072 | tf_op jit(solution)/shard_map/while/body/eval_jaxpr/ppermute | solution.py:18
  373.7 13.1 %collective-permute-start = (f32[8,153,128]{2,0,1:T(8,128)}, f32[8,153,128]{2,0,1:T(8,128)S(1)}, u32[]{:S(2)}, u32[]{:S(2)}) collective-permute-start(f32[8,153,128]{2,0,1:T(8,128)} %get-tuple-element.766), channel_id=1, source_target_pairs={{0,1},{1,2},{2,3},{3,4},{4,5},{5,6},{6,7},{7,8},{8,9},{9,10},{10,1... | collective-permute-start | bytes 1880072 | tf_op jit(solution)/shard_map/while/body/eval_jaxpr/ppermute | solution.py:18
  387.8 12.7 %collective-permute-start = (f32[8,153,128]{2,0,1:T(8,128)}, f32[8,153,128]{2,0,1:T(8,128)S(1)}, u32[]{:S(2)}, u32[]{:S(2)}) collective-permute-start(f32[8,153,128]{2,0,1:T(8,128)} %get-tuple-element.766), channel_id=1, source_target_pairs={{0,1},{1,2},{2,3},{3,4},{4,5},{5,6},{6,7},{7,8},{8,9},{9,10},{10,1... | collective-permute-start | bytes 1880072 | tf_op jit(solution)/shard_map/while/body/eval_jaxpr/ppermute | solution.py:18
  401.6 12.9 %collective-permute-start = (f32[8,153,128]{2,0,1:T(8,128)}, f32[8,153,128]{2,0,1:T(8,128)S(1)}, u32[]{:S(2)}, u32[]{:S(2)}) collective-permute-start(f32[8,153,128]{2,0,1:T(8,128)} %get-tuple-element.766), channel_id=1, source_target_pairs={{0,1},{1,2},{2,3},{3,4},{4,5},{5,6},{6,7},{7,8},{8,9},{9,10},{10,1... | collective-permute-start | bytes 1880072 | tf_op jit(solution)/shard_map/while/body/eval_jaxpr/ppermute | solution.py:18
  415.5 15.3 %collective-permute-start = (f32[8,153,128]{2,0,1:T(8,128)}, f32[8,153,128]{2,0,1:T(8,128)S(1)}, u32[]{:S(2)}, u32[]{:S(2)}) collective-permute-start(f32[8,153,128]{2,0,1:T(8,128)} %get-tuple-element.766), channel_id=1, source_target_pairs={{0,1},{1,2},{2,3},{3,4},{4,5},{5,6},{6,7},{7,8},{8,9},{9,10},{10,1... | collective-permute-start | bytes 1880072 | tf_op jit(solution)/shard_map/while/body/eval_jaxpr/ppermute | solution.py:18
  431.9 13.7 %collective-permute-start = (f32[8,153,128]{2,0,1:T(8,128)}, f32[8,153,128]{2,0,1:T(8,128)S(1)}, u32[]{:S(2)}, u32[]{:S(2)}) collective-permute-start(f32[8,153,128]{2,0,1:T(8,128)} %get-tuple-element.766), channel_id=1, source_target_pairs={{0,1},{1,2},{2,3},{3,4},{4,5},{5,6},{6,7},{7,8},{8,9},{9,10},{10,1... | collective-permute-start | bytes 1880072 | tf_op jit(solution)/shard_map/while/body/eval_jaxpr/ppermute | solution.py:18
  446.7 14.5 %collective-permute-start = (f32[8,153,128]{2,0,1:T(8,128)}, f32[8,153,128]{2,0,1:T(8,128)S(1)}, u32[]{:S(2)}, u32[]{:S(2)}) collective-permute-start(f32[8,153,128]{2,0,1:T(8,128)} %get-tuple-element.766), channel_id=1, source_target_pairs={{0,1},{1,2},{2,3},{3,4},{4,5},{5,6},{6,7},{7,8},{8,9},{9,10},{10,1... | collective-permute-start | bytes 1880072 | tf_op jit(solution)/shard_map/while/body/eval_jaxpr/ppermute | solution.py:18
  462.2 15.3 %collective-permute-start = (f32[8,153,128]{2,0,1:T(8,128)}, f32[8,153,128]{2,0,1:T(8,128)S(1)}, u32[]{:S(2)}, u32[]{:S(2)}) collective-permute-start(f32[8,153,128]{2,0,1:T(8,128)} %get-tuple-element.766), channel_id=1, source_target_pairs={{0,1},{1,2},{2,3},{3,4},{4,5},{5,6},{6,7},{7,8},{8,9},{9,10},{10,1... | collective-permute-start | bytes 1880072 | tf_op jit(solution)/shard_map/while/body/eval_jaxpr/ppermute | solution.py:18
  478.6 16.1 %collective-permute-start = (f32[8,153,128]{2,0,1:T(8,128)}, f32[8,153,128]{2,0,1:T(8,128)S(1)}, u32[]{:S(2)}, u32[]{:S(2)}) collective-permute-start(f32[8,153,128]{2,0,1:T(8,128)} %get-tuple-element.766), channel_id=1, source_target_pairs={{0,1},{1,2},{2,3},{3,4},{4,5},{5,6},{6,7},{7,8},{8,9},{9,10},{10,1... | collective-permute-start | bytes 1880072 | tf_op jit(solution)/shard_map/while/body/eval_jaxpr/ppermute | solution.py:18
  495.7 16.9 %collective-permute-start = (f32[8,153,128]{2,0,1:T(8,128)}, f32[8,153,128]{2,0,1:T(8,128)S(1)}, u32[]{:S(2)}, u32[]{:S(2)}) collective-permute-start(f32[8,153,128]{2,0,1:T(8,128)} %get-tuple-element.766), channel_id=1, source_target_pairs={{0,1},{1,2},{2,3},{3,4},{4,5},{5,6},{6,7},{7,8},{8,9},{9,10},{10,1... | collective-permute-start | bytes 1880072 | tf_op jit(solution)/shard_map/while/body/eval_jaxpr/ppermute | solution.py:18
  513.7 17.7 %collective-permute-start = (f32[8,153,128]{2,0,1:T(8,128)}, f32[8,153,128]{2,0,1:T(8,128)S(1)}, u32[]{:S(2)}, u32[]{:S(2)}) collective-permute-start(f32[8,153,128]{2,0,1:T(8,128)} %get-tuple-element.766), channel_id=1, source_target_pairs={{0,1},{1,2},{2,3},{3,4},{4,5},{5,6},{6,7},{7,8},{8,9},{9,10},{10,1... | collective-permute-start | bytes 1880072 | tf_op jit(solution)/shard_map/while/body/eval_jaxpr/ppermute | solution.py:18
  532.4 20.2 %collective-permute-start = (f32[8,153,128]{2,0,1:T(8,128)}, f32[8,153,128]{2,0,1:T(8,128)S(1)}, u32[]{:S(2)}, u32[]{:S(2)}) collective-permute-start(f32[8,153,128]{2,0,1:T(8,128)} %get-tuple-element.766), channel_id=1, source_target_pairs={{0,1},{1,2},{2,3},{3,4},{4,5},{5,6},{6,7},{7,8},{8,9},{9,10},{10,1... | collective-permute-start | bytes 1880072 | tf_op jit(solution)/shard_map/while/body/eval_jaxpr/ppermute | solution.py:18
  553.6 21.6 %collective-permute-start = (f32[8,153,128]{2,0,1:T(8,128)}, f32[8,153,128]{2,0,1:T(8,128)S(1)}, u32[]{:S(2)}, u32[]{:S(2)}) collective-permute-start(f32[8,153,128]{2,0,1:T(8,128)} %get-tuple-element.766), channel_id=1, source_target_pairs={{0,1},{1,2},{2,3},{3,4},{4,5},{5,6},{6,7},{7,8},{8,9},{9,10},{10,1... | collective-permute-start | bytes 1880072 | tf_op jit(solution)/shard_map/while/body/eval_jaxpr/ppermute | solution.py:18
  578.2 27.5 %copy-start.34 = (bf16[256,8,16]{0,2,1:T(8,128)(2,1)S(1)}, bf16[256,8,16]{0,2,1:T(8,128)(2,1)}, u32[]{:S(2)}) copy-start(bf16[256,8,16]{0,2,1:T(8,128)(2,1)} %get-tuple-element.550) | copy-start | bytes 196612
  609.2 80.6 %copy-start.18 = (bf16[256,8,128]{0,2,1:T(8,128)(2,1)}, bf16[256,8,128]{0,2,1:T(8,128)(2,1)S(1)}, u32[]{:S(2)}) copy-start(bf16[256,8,128]{0,2,1:T(8,128)(2,1)S(1)} %get-tuple-element.543) | copy-start | bytes 1572868
  609.7 80.2 %copy-start.19 = (bf16[8,153,128]{2,0,1:T(8,128)(2,1)S(1)}, bf16[8,153,128]{2,0,1:T(8,128)(2,1)}, u32[]{:S(2)}) copy-start(bf16[8,153,128]{2,0,1:T(8,128)(2,1)} %convert_element_type.155) | copy-start | bytes 940036
  691.5 87.4 %copy-start.55 = (bf16[32]{0:T(256)(128)(2,1)S(1)}, bf16[32]{0:T(256)(128)(2,1)}, u32[]{:S(2)}) copy-start(bf16[32]{0:T(256)(128)(2,1)} %all-reduce) | copy-start | bytes 196
  728.4 50.4 %copy-start.16 = (f32[8,256,128]{1,2,0:T(8,128)}, f32[8,256,128]{1,2,0:T(8,128)S(1)}, u32[]{:S(2)}) copy-start(f32[8,256,128]{1,2,0:T(8,128)S(1)} %get-tuple-element.319) | copy-start | bytes 3145732
  778.9 77.0 %copy-start.25 = (bf16[32,8,8,128]{3,2,1,0:T(8,128)(2,1)S(1)}, bf16[32,8,8,128]{3,2,1,0:T(8,128)(2,1)}, u32[]{:S(2)}) copy-start(bf16[32,8,8,128]{3,2,1,0:T(8,128)(2,1)} %fusion.62) | copy-start | bytes 1572868
  867.0 11.8 %copy-start.41 = (s32[136]{0:T(256)S(1)}, s32[136]{0:T(256)}, u32[]{:S(2)}) copy-start(s32[136]{0:T(256)} %constant.186) | copy-start | bytes 1636
  878.8 6.2 copy-start.36
  900.3 5.9 copy-start.35
  900.3 8.1 copy-start.23
  907.1 4.4 collective-permute-start.2
  (74 other events, 123.2 us)
Sparse Core Ops, SparseCore 0:
  610.7 168.0 all-gather.2
where the time goes:
time: 1000 us; the launch traced here: 999 us
  waiting for transfers between devices  374 us (37%)
  starting transfers between devices  182 us (18%)
  blocking collectives  155 us (16%)
  other arithmetic  105 us (10%)
  local copies, waits for them, and re-layouts  82.4 us (8%)
  matrix products  62.1 us (6%)
  loops' own time  22.1 us (2%)
  between operations  16.2 us (2%)
    ppermute x34, waiting for transfers between devices, from_behind(): lax.ppermute(value, axis, [(source, source + steps) for source in range(i...  324 us
    ppermute x34, starting transfers between devices, from_behind(): lax.ppermute(value, axis, [(source, source + steps) for source in range(i...  182 us
    unnamed x1, blocking collectives  77.9 us
    psum x1, blocking collectives, shards(): lax.psum((conv_grad_query, conv_grad_key, conv_grad_value, gain_part), ('...  77.5 us
    all_gather x1, waiting for transfers between devices, entering(): lax.all_gather(a.astype(kind), axis)  50.4 us
    dynamic_slice x62, local copies, waits for them, and re-layouts, one(): lax.dynamic_index_in_dim(a, source, 0, False).astype(own.dtype)  49.1 us
    scatter-add x4, other arithmetic, features(): pairs = units[..., upper_rows] * units[..., upper_cols] * weight  35.8 us
    add x32, other arithmetic, relay_step(): return (received, tail + (1.0 - reset) * received)  31.5 us
  transfers between devices with their start and end apart: 35, of which 34 were waited for; matrix products, arithmetic and copies ran while one was open for 5% of the time, Pallas kernels for 0%

commit v1 on v0

v1 whole, which is shorter than its diff:
```python
import functools

import jax
import jax.numpy as jnp
from jax import lax
from jax.experimental import pallas as pl
from jax.experimental.pallas import tpu as pltpu
from jax.sharding import PartitionSpec as P

HEADS = 8
F = 16
HD = 128
T = 256
DOCS = 8
ROWS = 160
ZN = 8
EPS = 1e-06
MESH = pl.DeviceIdType.MESH
F32 = jnp.float32
BF16 = jnp.bfloat16


def dot(a, b, ca, cb):
    return lax.dot_general(a, b, (((ca,), (cb,)), ((), ())), preferred_element_type=F32)


def turned(u, d):
    return pltpu.roll(u, F - d, 0) if d else u


def put_features(out, h, u, ones):
    out[h, 0:16, :] = (u * u * (0.5**0.5)).astype(BF16)
    for d in range(1, 8):
        out[h, 16 * d : 16 * d + 16, :] = (u * turned(u, d)).astype(BF16)
    out[h, 128:144, :] = u.astype(BF16)
    rest = jnp.where(lax.broadcasted_iota(jnp.int32, (8, T), 0) == 0, ones, 0.0)
    out[h, 144:160, :] = jnp.concatenate([u[0:8] * u[8:16], rest], axis=0).astype(BF16)


def pull_features(g, u, ones):
    total = g[128:144] * ones + (2.0 * 0.5**0.5) * g[0:16] * u
    for d in range(1, 8):
        own = g[16 * d : 16 * d + 16]
        total = total + own * turned(u, d) + pltpu.roll(own * u, d, 0)
    half = g[144:152]
    total = total + jnp.concatenate([half * u[8:16], half * u[0:8]], axis=0)
    return 0.5 * total


def kernel(
    n_dp,
    n_ctx,
    lens,
    q_ref,
    k_ref,
    v_ref,
    og_ref,
    wq_ref,
    wk_ref,
    wv_ref,
    gain_ref,
    mixed_ref,
    gq_ref,
    gk_ref,
    gv_ref,
    gwq_ref,
    gwk_ref,
    gwv_ref,
    gg_ref,
    xq,
    xk,
    xv,
    qc,
    kc,
    qt,
    kt,
    uq,
    uk,
    vc,
    mask_ref,
    kern,
    saved,
    inner,
    phiq,
    phik,
    ga_ref,
    gvs,
    gqt,
    gkt,
    gqs,
    gks,
    local,
    halo_q,
    halo_k,
    halo_v,
    back_q,
    back_k,
    back_v,
    tail1,
    got1,
    tot1,
    ytot1,
    send1,
    inc,
    tail2,
    got2,
    tot2,
    ytot2,
    send2,
    outg,
    part,
    red_z,
    one_z,
    red_y,
    one_y,
    red_d,
    one_d,
    all_z,
    halo_ss,
    halo_rs,
    back_ss,
    back_rs,
    a_ss,
    a_rs,
    y_ss,
    y_rs,
    b_ss,
    b_rs,
    rz_ss,
    rz_rs,
    ry_ss,
    ry_rs,
    rd_ss,
    rd_rs,
    az_ss,
    az_rs,
):
    n_y = n_ctx // ZN
    me = lax.axis_index("ctx")
    dp = lax.axis_index("dp")
    y = me // ZN
    z = me % ZN
    after = (me + 1) % n_ctx
    before = (me + n_ctx - 1) % n_ctx

    def z_peer(zz):
        return {"ctx": y * ZN + zz}

    def y_peer(yy):
        return {"ctx": yy * ZN + z}

    barrier = pltpu.get_barrier_semaphore()
    greeted = [z_peer((z + j) % ZN) for j in range(1, ZN)]
    greeted += [y_peer((y + j) % n_y) for j in range(1, n_y)]
    greeted += [{"dp": (dp + j) % n_dp} for j in range(1, n_dp)]
    greeted += [{"ctx": after}, {"ctx": before}]
    for peer in greeted:
        pl.semaphore_signal(barrier, inc=1, device_id=peer, device_id_type=MESH)

    starts = []
    total = jnp.int32(0)
    for d in range(DOCS):
        starts.append(total)
        total = total + lens[0, d]
    first = me * T

    def doc_of(position):
        found = jnp.where(position >= starts[0], 1, 0)
        for d in range(1, DOCS):
            found = found + jnp.where(position >= starts[d], 1, 0)
        return found

    row_pos = first + lax.broadcasted_iota(jnp.int32, (1, T), 1)
    col_pos = first + lax.broadcasted_iota(jnp.int32, (T, 1), 0)
    row_doc, col_doc = doc_of(row_pos), doc_of(col_pos)
    prev_doc, last_doc = doc_of(first - 1), doc_of(first + T - 1)
    use_prev = jnp.where(row_doc == prev_doc, 1.0, 0.0)
    use_next = jnp.where(row_doc == last_doc, 1.0, 0.0)
    mask_ref[...] = jnp.where((row_pos <= col_pos) & (row_doc == col_doc), 1.0, 0.0)

    def keep_of(block):
        value = jnp.float32(1.0)
        for d in range(DOCS):
            value = jnp.where(starts[d] // T == block, 0.0, value)
        return value

    def keep_group(group):
        value = jnp.float32(1.0)
        for d in range(DOCS):
            value = jnp.where(starts[d] // (T * ZN) == group, 0.0, value)
        return value

    xq[8:, :] = q_ref[...].astype(F32)
    xk[8:, :] = k_ref[...].astype(F32)
    for h in range(HEADS):
        xv[h, 8:, :] = v_ref[:, h * HD : (h + 1) * HD].astype(F32)

    pl.semaphore_wait(barrier, len(greeted))

    def remote(src, dst, ss, rs, peer):
        return pltpu.make_async_remote_copy(
            src_ref=src, dst_ref=dst, send_sem=ss, recv_sem=rs, device_id=peer, device_id_type=MESH
        )

    halos = [
        remote(ref.at[T - 16 :, :], dst, halo_ss.at[i], halo_rs.at[i], {"ctx": after})
        for i, (ref, dst) in enumerate([(q_ref, halo_q), (k_ref, halo_k), (v_ref, halo_v)])
    ]
    for c in halos:
        c.start()
    for c in halos:
        c.wait_recv()
    inside = jnp.where(me > 0, 1.0, 0.0)
    xq[0:8, :] = halo_q[...].astype(F32)[8:16] * inside
    xk[0:8, :] = halo_k[...].astype(F32)[8:16] * inside
    for h in range(HEADS):
        xv[h, 0:8, :] = halo_v[:, h * HD : (h + 1) * HD].astype(F32)[8:16] * inside

    def conv(x, w):
        return w[0:1] * x[8 : 8 + T] + w[1:2] * x[7 : 7 + T] + w[2:3] * x[6 : 6 + T]

    q = conv(xq, wq_ref[...]).astype(BF16)
    k = conv(xk, wk_ref[...]).astype(BF16)
    qc[...] = q
    kc[...] = k
    q_turned = q.astype(F32).T
    k_turned = k.astype(F32).T
    qt[...] = q_turned.astype(BF16)
    kt[...] = k_turned.astype(BF16)
    uq[...] = q_turned * (0.5 * use_prev)
    uk[...] = k_turned * (0.5 * use_next)

    def head_rows(h):
        return pl.ds(pl.multiple_of(h * F, F), F)

    def head_cols(h):
        return pl.ds(pl.multiple_of(h * HD, HD), HD)

    def a_copy(tail, got, phase, h):
        return remote(
            tail.at[h], got.at[z], a_ss.at[phase, h], a_rs.at[phase, z], z_peer(h)
        )

    def a_arrival(tail, got, phase, zz):
        return remote(
            tail.at[zz], got.at[zz], a_ss.at[phase, zz], a_rs.at[phase, zz], z_peer(zz)
        )

    def b_copy(send, take, phase, zz):
        return remote(send.at[zz], take.at[z], b_ss.at[phase, zz], b_rs.at[phase, z], z_peer(zz))

    def b_arrival(send, take, phase, h):
        return remote(send.at[h], take.at[h], b_ss.at[phase, h], b_rs.at[phase, h], z_peer(h))

    def tail_head(h):
        cols = head_cols(h)
        w = wv_ref[:, cols]
        x = xv.at[h]
        value = (
            w[0:1] * x[8 : 8 + T, :] + w[1:2] * x[7 : 7 + T, :] + w[2:3] * x[6 : 6 + T, :]
        ).astype(BF16)
        vc[h] = value
        put_features(phik, h, uk[head_rows(h), :], use_next)
        tail1[h] = dot(phik[h], value, 1, 0).astype(BF16)

    def tail_step(j, _):
        h = (z + 1 + j) % ZN
        tail_head(h)
        a_copy(tail1, got1, 0, h).start()
        return 0

    lax.fori_loop(0, ZN - 1, tail_step, 0)
    tail_head(z)
    got1[z] = tail1[z]

    lane_head = lax.broadcasted_iota(jnp.int32, (1, HEADS * F), 1) // F

    def inner_step(h, _):
        chosen = jnp.where(lane_head == h, 0.25, 0.0).astype(BF16)
        scores = dot(qc[...] * chosen, kc[...], 1, 1)
        m = mask_ref[...]
        kernel_h = (m * (1.0 + scores + 0.5 * scores * scores)).astype(BF16)
        kern[h] = kernel_h
        saved[h] = m * (1.0 + scores)
        inner[h] = dot(kernel_h, vc[h], 1, 0)
        put_features(phiq, h, uq[head_rows(h), :], use_prev)
        return 0

    lax.fori_loop(0, HEADS, inner_step, 0)

    def scan(tail, got, tot, ytot, send, take, phase, reverse):
        def wait_a(j, _):
            a_arrival(tail, got, phase, (z + j) % ZN).wait_recv()
            return 0

        lax.fori_loop(1, ZN, wait_a, 0)
        order = range(ZN - 1, -1, -1) if reverse else range(ZN)
        running = jnp.zeros((ROWS, HD), F32)
        keeps = {}
        for i in order:
            keeps[i] = keep_of(y * ZN + i)
            running = got[i].astype(F32) + keeps[i] * running
        tot[...] = running.astype(BF16)
        ytot[y] = running.astype(BF16)

        def y_copy(j):
            yy = (y + j) % n_y
            return remote(tot, ytot.at[y], y_ss.at[phase, yy], y_rs.at[phase, y], y_peer(yy))

        def y_arrival(j):
            yy = (y + j) % n_y
            return remote(tot, ytot.at[yy], y_ss.at[phase, yy], y_rs.at[phase, yy], y_peer(yy))

        for j in range(1, n_y):
            y_copy(j).start()
        for j in range(1, n_y):
            y_arrival(j).wait_recv()
        carry = jnp.zeros((ROWS, HD), F32)
        for g in range(n_y - 1, 0, -1) if reverse else range(n_y - 1):
            counts = jnp.where(g > y if reverse else g < y, 1.0, 0.0)
            onward = ytot[g].astype(F32) + keep_group(g) * carry
            carry = counts * onward + (1.0 - counts) * carry
        running = carry
        for i in order:
            send[i] = running.astype(BF16)
            running = got[i].astype(F32) + keeps[i] * running

        def send_b(j, _):
            b_copy(send, take, phase, (z + j) % ZN).start()
            return 0

        lax.fori_loop(1, ZN, send_b, 0)
        take[z] = send[z]

    scan(tail1, got1, tot1, ytot1, send1, inc, 0, False)

    def forward_head(h):
        cols = head_cols(h)
        attended = inner[h] + dot(phiq[h], inc[h], 0, 0)
        r = lax.rsqrt(jnp.mean(attended * attended, axis=-1, keepdims=True) + EPS)
        normed = attended * r
        gains = gain_ref[:, cols]
        mixed_ref[:, cols] = (normed * gains).astype(BF16)
        upstream = og_ref[:, cols].astype(F32)
        local[h, 3:4, :] = jnp.sum(upstream * normed, axis=0, keepdims=True)
        pulled = upstream * gains
        along = jnp.mean(pulled * normed, axis=-1, keepdims=True)
        grad = ((pulled - normed * along) * r).astype(BF16)
        ga_ref[h] = grad
        tail2[h] = dot(phiq[h], grad, 1, 0).astype(BF16)

    local[...] = jnp.zeros(local.shape, F32)
    forward_head(z)
    got2[z] = tail2[z]

    def nearest(j):
        away = (j + 1) // 2
        return (z + ZN + away * (1 - 2 * (j % 2))) % ZN

    def forward_step(j, _):
        h = nearest(j)
        b_arrival(send1, inc, 0, h).wait_recv()
        forward_head(h)
        a_copy(tail2, got2, 1, h).start()
        return 0

    lax.fori_loop(1, ZN, forward_step, 0)

    def backward_step(h, _):
        grad = ga_ref[h]
        grad_scores = (dot(grad, vc[h], 1, 1) * saved[h]).astype(BF16)
        rows = head_rows(h)
        grad_phi = dot(inc[h], grad, 1, 1)
        gqt[rows, :] = 0.25 * dot(kt[rows, :], grad_scores, 1, 1) + pull_features(
            grad_phi, uq[rows, :], use_prev
        )
        gkt[rows, :] = 0.25 * dot(qt[rows, :], grad_scores, 1, 0)
        gvs[h, 0:T, :] = dot(kern[h], grad, 0, 0)
        return 0

    lax.fori_loop(0, HEADS, backward_step, 0)

    scan(tail2, got2, tot2, ytot2, send2, outg, 1, True)

    def taps(g, x):
        return [jnp.sum(g * x[8 - j : 8 - j + T], axis=0, keepdims=True) for j in range(3)]

    def last_head(h):
        rows = head_rows(h)
        later = outg[h]
        grad_phi = dot(later, vc[h], 1, 1)
        gkt[rows, :] = gkt[rows, :] + pull_features(grad_phi, uk[rows, :], use_next)
        g = gvs[h, 0:T, :] + dot(phik[h], later, 0, 0)
        gvs[h, 0:T, :] = g
        for j in range(3):
            local[h, j : j + 1, :] = jnp.sum(
                g * xv[h, 8 - j : 8 - j + T, :], axis=0, keepdims=True
            )

    last_head(z)

    def last_step(j, _):
        h = nearest(j)
        b_arrival(send2, outg, 1, h).wait_recv()
        last_head(h)
        return 0

    lax.fori_loop(1, ZN, last_step, 0)
    gq = gqt[...].T
    gk = gkt[...].T
    gqs[0:T, :] = gq
    gks[0:T, :] = gk

    backs = [
        remote(src, dst, back_ss.at[i], back_rs.at[i], {"ctx": before})
        for i, (src, dst) in enumerate(
            [
                (gqs.at[0:8, :], back_q),
                (gks.at[0:8, :], back_k),
                (gvs.at[:, 0:8, :], back_v),
            ]
        )
    ]
    for c in backs:
        c.start()

    for j in range(3):
        local[0, 4 + j : 5 + j, :] = jnp.sum(gq * xq[8 - j : 8 - j + T, :], axis=0, keepdims=True)
        local[1, 4 + j : 5 + j, :] = jnp.sum(gk * xk[8 - j : 8 - j + T, :], axis=0, keepdims=True)

    def rz_copy(zz):
        return remote(local.at[zz], red_z.at[z], rz_ss.at[zz], rz_rs.at[z], z_peer(zz))

    def rz_arrival(zz):
        return remote(local.at[zz], red_z.at[zz], rz_ss.at[zz], rz_rs.at[zz], z_peer(zz))

    for j in range(1, ZN):
        rz_copy((z + j) % ZN).start()
    red_z[z] = local[z]

    for c in backs:
        c.wait_recv()
    inside_next = jnp.where(me < n_ctx - 1, 1.0, 0.0)
    gqs[T : T + 8, :] = back_q[...] * inside_next
    gks[T : T + 8, :] = back_k[...] * inside_next
    for c in backs:
        c.wait_send()
    gvs[:, T : T + 8, :] = back_v[...] * inside_next

    def conv_back(g, w):
        return (w[0:1] * g[0:T] + w[1:2] * g[1 : 1 + T] + w[2:3] * g[2 : 2 + T]).astype(BF16)

    gq_ref[...] = conv_back(gqs, wq_ref[...])
    gk_ref[...] = conv_back(gks, wk_ref[...])

    def value_step(h, _):
        cols = head_cols(h)
        w = wv_ref[:, cols]
        gv_ref[:, cols] = (
            w[0:1] * gvs[h, 0:T, :]
            + w[1:2] * gvs[h, 1 : 1 + T, :]
            + w[2:3] * gvs[h, 2 : 2 + T, :]
        ).astype(BF16)
        return 0

    lax.fori_loop(0, HEADS, value_step, 0)

    for j in range(1, ZN):
        rz_arrival((z + j) % ZN).wait_recv()
    tile = jnp.sum(red_z[...], axis=0)
    one_y[...] = tile
    red_y[y] = tile

    def ry(yy, slot):
        return remote(one_y, red_y.at[slot], ry_ss.at[yy], ry_rs.at[slot], y_peer(yy))

    for j in range(1, n_y):
        ry((y + j) % n_y, y).start()
    for j in range(1, n_y):
        ry((y + j) % n_y, (y + j) % n_y).wait_recv()
    tile = jnp.sum(red_y[...], axis=0)
    one_d[...] = tile
    red_d[dp] = tile

    def rd(dd, slot):
        return remote(one_d, red_d.at[slot], rd_ss.at[dd], rd_rs.at[slot], {"dp": dd})

    for j in range(1, n_dp):
        rd((dp + j) % n_dp, dp).start()
    for j in range(1, n_dp):
        rd((dp + j) % n_dp, (dp + j) % n_dp).wait_recv()
    tile = jnp.sum(red_d[...], axis=0)
    one_z[...] = tile
    all_z[z] = tile

    def az(zz, slot):
        return remote(one_z, all_z.at[slot], az_ss.at[zz], az_rs.at[slot], z_peer(zz))

    for j in range(1, ZN):
        az((z + j) % ZN, z).start()
    for j in range(1, ZN):
        az((z + j) % ZN, (z + j) % ZN).wait_recv()
    gwq_ref[...] = all_z[0, 4:7, :]
    gwk_ref[...] = all_z[1, 4:7, :]
    for h in range(HEADS):
        gwv_ref[:, h * HD : (h + 1) * HD] = all_z[h, 0:3, :]
        gg_ref[:, h * HD : (h + 1) * HD] = all_z[h, 3:4, :]

    for c in halos:
        c.wait_send()

    def left(j, _):
        zz = (z + j) % ZN
        a_copy(tail1, got1, 0, zz).wait_send()
        a_copy(tail2, got2, 1, zz).wait_send()
        b_copy(send1, inc, 0, zz).wait_send()
        b_copy(send2, outg, 1, zz).wait_send()
        rz_copy(zz).wait_send()
        az(zz, z).wait_send()
        return 0

    lax.fori_loop(1, ZN, left, 0)
    for j in range(1, n_y):
        yy = (y + j) % n_y
        remote(tot1, ytot1.at[y], y_ss.at[0, yy], y_rs.at[0, y], y_peer(yy)).wait_send()
        remote(tot2, ytot2.at[y], y_ss.at[1, yy], y_rs.at[1, y], y_peer(yy)).wait_send()
        ry(yy, y).wait_send()
    for j in range(1, n_dp):
        rd((dp + j) % n_dp, dp).wait_send()


def solution(mesh):
    n_dp, n_ctx = mesh.shape["dp"], mesh.shape["ctx"]
    n_y = n_ctx // ZN
    wide = HEADS * HD
    thin = HEADS * F

    def shards(q, k, v, wq, wk, wv, gain, lens, og):
        vmem = pl.BlockSpec(memory_space=pltpu.VMEM)
        state = (ROWS, HD)
        scratch = [
            pltpu.VMEM((T + 8, thin), F32),
            pltpu.VMEM((T + 8, thin), F32),
            pltpu.VMEM((HEADS, T + 8, HD), F32),
            pltpu.VMEM((T, thin), BF16),
            pltpu.VMEM((T, thin), BF16),
            pltpu.VMEM((thin, T), BF16),
            pltpu.VMEM((thin, T), BF16),
            pltpu.VMEM((thin, T), F32),
            pltpu.VMEM((thin, T), F32),
            pltpu.VMEM((HEADS, T, HD), BF16),
            pltpu.VMEM((T, T), F32),
            pltpu.VMEM((HEADS, T, T), BF16),
            pltpu.VMEM((HEADS, T, T), F32),
            pltpu.VMEM((HEADS, T, HD), F32),
            pltpu.VMEM((HEADS, ROWS, T), BF16),
            pltpu.VMEM((HEADS, ROWS, T), BF16),
            pltpu.VMEM((HEADS, T, HD), BF16),
            pltpu.VMEM((HEADS, T + 8, HD), F32),
            pltpu.VMEM((thin, T), F32),
            pltpu.VMEM((thin, T), F32),
            pltpu.VMEM((T + 8, thin), F32),
            pltpu.VMEM((T + 8, thin), F32),
            pltpu.VMEM((HEADS, 8, HD), F32),
            pltpu.VMEM((16, thin), BF16),
            pltpu.VMEM((16, thin), BF16),
            pltpu.VMEM((16, wide), BF16),
            pltpu.VMEM((8, thin), F32),
            pltpu.VMEM((8, thin), F32),
            pltpu.VMEM((HEADS, 8, HD), F32),
        ]
        for _ in range(2):
            scratch += [
                pltpu.VMEM((HEADS,) + state, BF16),
                pltpu.VMEM((ZN,) + state, BF16),
                pltpu.VMEM(state, BF16),
                pltpu.VMEM((n_y,) + state, BF16),
                pltpu.VMEM((ZN,) + state, BF16),
                pltpu.VMEM((HEADS,) + state, BF16),
            ]
        tile = (8, HD)
        scratch += [
            pltpu.VMEM(tile, F32),
            pltpu.VMEM((ZN,) + tile, F32),
            pltpu.VMEM(tile, F32),
            pltpu.VMEM((n_y,) + tile, F32),
            pltpu.VMEM(tile, F32),
            pltpu.VMEM((n_dp,) + tile, F32),
            pltpu.VMEM(tile, F32),
            pltpu.VMEM((ZN,) + tile, F32),
        ]
        dma = pltpu.SemaphoreType.DMA
        for counts in ((3,), (3,), (2, ZN), (2, n_y), (2, ZN), (ZN,), (n_y,), (n_dp,), (ZN,)):
            scratch += [dma(counts), dma(counts)]
        outs = pl.pallas_call(
            functools.partial(kernel, n_dp, n_ctx),
            out_shape=(
                jax.ShapeDtypeStruct((T, wide), BF16),
                jax.ShapeDtypeStruct((T, thin), BF16),
                jax.ShapeDtypeStruct((T, thin), BF16),
                jax.ShapeDtypeStruct((T, wide), BF16),
                jax.ShapeDtypeStruct((3, thin), F32),
                jax.ShapeDtypeStruct((3, thin), F32),
                jax.ShapeDtypeStruct((3, wide), F32),
                jax.ShapeDtypeStruct((1, wide), F32),
            ),
            in_specs=[pl.BlockSpec(memory_space=pltpu.SMEM)] + [vmem] * 8,
            out_specs=(vmem,) * 8,
            scratch_shapes=scratch,
            compiler_params=pltpu.CompilerParams(
                collective_id=0, has_side_effects=True, vmem_limit_bytes=48 * 2**20
            ),
        )(lens, q[0], k[0], v[0], og[0], wq, wk, wv, gain[None])
        mixed, gq, gk, gv, gwq, gwk, gwv, gg = outs
        return mixed[None], gq[None], gk[None], gv[None], gwq, gwk, gwv, gg[0]

    tokens = P("dp", "ctx", None)
    return jax.shard_map(
        shards,
        mesh=mesh,
        in_specs=(tokens, tokens, tokens, P(), P(), P(), P(), P("dp", None), tokens),
        out_specs=(tokens, tokens, tokens, tokens, P(), P(), P(), P()),
        check_vma=False,
    )
```

time: 1000 us -> 87.1 us (0.09)
  waiting for transfers between devices: 374 us -> 0 us
  starting transfers between devices: 182 us -> 0 us
  blocking collectives: 155 us -> 0 us
  other arithmetic: 105 us -> 0 us
  Pallas kernels: 0 us -> 75.7 us
  local copies, waits for them, and re-layouts: 82.4 us -> 10.4 us
  matrix products: 62.1 us -> 0 us
  loops' own time: 22.1 us -> 0 us
  between operations: 16.2 us -> 0.69 us
    ppermute x34 -> x0, waiting for transfers between devices: 324 us -> none  [from_behind(): lax.ppermute(value, axis, [(source, source + steps) for source in range(i...]
    ppermute x34 -> x0, starting transfers between devices: 182 us -> none  [from_behind(): lax.ppermute(value, axis, [(source, source + steps) for source in range(i...]
    unnamed x1 -> x0, blocking collectives: 77.9 us -> none
    psum x1 -> x0, blocking collectives: 77.5 us -> none  [shards(): lax.psum((conv_grad_query, conv_grad_key, conv_grad_value, gain_part), ('...]
    pallas_call x0 -> x1, Pallas kernels: none -> 75.7 us  [shards(): pl.pallas_call(functools.partial(kernel, n_dp, n_ctx), out_shape=(jax.Sha...]
    dot_general x54 -> x0, matrix products: 62.1 us -> none  [the longest x8 12.7 us: head_kernel(): jnp.dot(query_head, key_head.T, preferred_element_type=jnp.float32) * 0.25]
    all_gather x1 -> x0, waiting for transfers between devices: 50.4 us -> none  [entering(): lax.all_gather(a.astype(kind), axis)]
    dynamic_slice x62 -> x0, local copies, waits for them, and re-layouts: 49.1 us -> none  [one(): lax.dynamic_index_in_dim(a, source, 0, False).astype(own.dtype)]
  transfers between devices with their start and end apart: 35 -> 0, of which waited for: 34 -> 0; matrix products, arithmetic and copies ran while one was open for 5% -> 0% of each run, Pallas kernels for 0% -> 0%
where the time goes in v1:
time: 87.1 us; the launch traced here: 86.8 us
  Pallas kernels  75.7 us (87%)
  local copies, waits for them, and re-layouts  10.4 us (12%)
    pallas_call x1, Pallas kernels, shards(): pl.pallas_call(functools.partial(kernel, n_dp, n_ctx), out_shape=(jax.Sha...  75.7 us
    unnamed x26, local copies, waits for them, and re-layouts  10.4 us

profile of v1, /device:TPU:1, one launch (start us, length us, event | category | flops | bytes accessed | tf_op | source)
XLA Modules:
  0.0 86.8 jit_solution(15533609718814876874)
XLA Ops:
  0.6 0.0 copy-start.7
  0.6 0.0 copy-start.5
  0.7 0.0 copy-start.6
  0.7 0.0 copy-start.8
  0.7 0.6 copy-done.7
  1.3 0.0 copy-done.5
  1.3 0.0 copy-done.6
  1.4 0.0 copy-done.8
  1.4 0.0 copy-start
  1.4 1.0 %copy-done = bf16[1,256,1024]{2,1,0:T(8,128)(2,1)S(1)} copy-done((bf16[1,256,1024]{2,1,0:T(8,128)(2,1)S(1)}, bf16[1,256,1024]{2,1,0:T(8,128)(2,1)}, u32[]{:S(2)}) %copy-start) | copy-done | bytes 524312
  2.4 0.0 copy-start.1
  2.4 1.0 %copy-done.1 = bf16[1,256,1024]{2,1,0:T(8,128)(2,1)S(1)} copy-done((bf16[1,256,1024]{2,1,0:T(8,128)(2,1)S(1)}, bf16[1,256,1024]{2,1,0:T(8,128)(2,1)}, u32[]{:S(2)}) %copy-start.1) | copy-done | bytes 524312
  3.4 0.0 copy-start.2
  3.4 0.8 copy-done.2
  4.3 0.0 copy-start.3
  4.3 0.8 copy-done.3
  5.1 0.0 copy-start.4
  5.1 0.7 copy-done.4
  5.8 75.7 %shard_map.152 = (bf16[256,1024]{1,0:T(8,128)(2,1)S(1)}, bf16[256,128]{1,0:T(8,128)(2,1)S(1)}, bf16[256,128]{1,0:T(8,128)(2,1)S(1)}, bf16[256,1024]{1,0:T(8,128)...) custom-call(s32[1,8]{1,0:T(1,128)S(1)} %copy-done.8, ...), custom_call_target="tpu_custom_call" | custom-call | tf_op jit(solution)/shard_map/pallas_call | solution.py:595
  81.6 0.8 copy.25
  82.4 0.6 copy.26
  83.0 0.6 copy.27
  83.6 0.8 copy.28
  84.4 0.6 copy.29
  85.0 0.6 copy.30
  85.6 0.6 copy.31
  86.2 0.6 copy.32
Async XLA Ops:
  0.6 0.7 copy-start.7
  0.6 0.7 copy-start.5
  0.7 0.7 copy-start.6
  0.7 0.7 copy-start.8
  1.4 1.0 %copy-start = (bf16[1,256,1024]{2,1,0:T(8,128)(2,1)S(1)}, bf16[1,256,1024]{2,1,0:T(8,128)(2,1)}, u32[]{:S(2)}) copy-start(bf16[1,256,1024]{2,1,0:T(8,128)(2,1)} %param.11) | copy-start | bytes 1572868
  2.4 1.0 %copy-start.1 = (bf16[1,256,1024]{2,1,0:T(8,128)(2,1)S(1)}, bf16[1,256,1024]{2,1,0:T(8,128)(2,1)}, u32[]{:S(2)}) copy-start(bf16[1,256,1024]{2,1,0:T(8,128)(2,1)} %param.17) | copy-start | bytes 1572868
  3.4 0.8 copy-start.2
  4.3 0.8 copy-start.3
  5.1 0.7 copy-start.4

commit v2 on v1

--- a/solution.py
+++ b/solution.py
@@ -50,6 +50,25 @@
 def kernel(
     n_dp,
     n_ctx,
+    lens_hbm,
+    q_hbm,
+    k_hbm,
+    v_hbm,
+    og_hbm,
+    wq_hbm,
+    wk_hbm,
+    wv_hbm,
+    gain_hbm,
+    mixed_hbm,
+    gq_hbm,
+    gk_hbm,
+    gv_hbm,
+    sums_ref,
+    mixed_ref,
+    gq_ref,
+    gk_ref,
+    gv_ref,
+    out_s,
     lens,
     q_ref,
     k_ref,
@@ -59,14 +78,6 @@
     wk_ref,
     wv_ref,
     gain_ref,
-    mixed_ref,
-    gq_ref,
-    gk_ref,
-    gv_ref,
-    gwq_ref,
-    gwk_ref,
-    gwv_ref,
-    gg_ref,
     xq,
     xk,
     xv,
@@ -108,14 +119,14 @@
     ytot2,
     send2,
     outg,
-    part,
+    halves,
+    red_c,
+    red_xy,
+    one_xy,
     red_z,
     one_z,
-    red_y,
-    one_y,
-    red_d,
-    one_d,
-    all_z,
+    one_c,
+    in_s,
     halo_ss,
     halo_rs,
     back_ss,
@@ -126,18 +137,21 @@
     y_rs,
     b_ss,
     b_rs,
+    rc_ss,
+    rc_rs,
+    rxy_ss,
+    rxy_rs,
     rz_ss,
     rz_rs,
-    ry_ss,
-    ry_rs,
-    rd_ss,
-    rd_rs,
-    az_ss,
-    az_rs,
+    ac_ss,
+    ac_rs,
 ):
     n_y = n_ctx // ZN
     me = lax.axis_index("ctx")
     dp = lax.axis_index("dp")
+    n_x = n_dp // 2
+    core = dp % 2
+    x = dp // 2
     y = me // ZN
     z = me % ZN
     after = (me + 1) % n_ctx
@@ -151,11 +165,37 @@
 
     barrier = pltpu.get_barrier_semaphore()
     greeted = [z_peer((z + j) % ZN) for j in range(1, ZN)]
-    greeted += [y_peer((y + j) % n_y) for j in range(1, n_y)]
-    greeted += [{"dp": (dp + j) % n_dp} for j in range(1, n_dp)]
-    greeted += [{"ctx": after}, {"ctx": before}]
+    other = {"dp": dp + 1 - 2 * core}
+    plane = []
+    for j in range(1, n_x * n_y):
+        xx = (x + j // n_y) % n_x
+        yy = (y + j % n_y) % n_y
+        plane.append((xx * n_y + yy, {"dp": xx * 2 + core, "ctx": yy * ZN + z}))
+    greeted += [peer for _, peer in plane]
+    greeted += [other, {"ctx": after}, {"ctx": before}]
     for peer in greeted:
         pl.semaphore_signal(barrier, inc=1, device_id=peer, device_id_type=MESH)
+
+    loads = [
+        pltpu.make_async_copy(src, dst, in_s.at[i])
+        for i, (src, dst) in enumerate(
+            [
+                (lens_hbm, lens),
+                (q_hbm, q_ref),
+                (k_hbm, k_ref),
+                (wq_hbm, wq_ref),
+                (wk_hbm, wk_ref),
+                (v_hbm, v_ref),
+                (wv_hbm, wv_ref),
+                (gain_hbm, gain_ref),
+                (og_hbm, og_ref),
+            ]
+        )
+    ]
+    for c in loads:
+        c.start()
+    for c in loads[:5]:
+        c.wait()
 
     starts = []
     total = jnp.int32(0)
@@ -190,10 +230,44 @@
             value = jnp.where(starts[d] // (T * ZN) == group, 0.0, value)
         return value
 
+    def conv(xs, w, rows):
+        return (
+            w[0:1] * xs[8 : 8 + rows, :] + w[1:2] * xs[7 : 7 + rows, :] + w[2:3] * xs[6 : 6 + rows, :]
+        ).astype(BF16)
+
+    def head_rows(h):
+        return pl.ds(pl.multiple_of(h * F, F), F)
+
+    def head_cols(h):
+        return pl.ds(pl.multiple_of(h * HD, HD), HD)
+
+    xq[0:8, :] = jnp.zeros((8, HEADS * F), F32)
+    xk[0:8, :] = jnp.zeros((8, HEADS * F), F32)
     xq[8:, :] = q_ref[...].astype(F32)
     xk[8:, :] = k_ref[...].astype(F32)
-    for h in range(HEADS):
-        xv[h, 8:, :] = v_ref[:, h * HD : (h + 1) * HD].astype(F32)
+    qc[...] = conv(xq, wq_ref[...], T)
+    kc[...] = conv(xk, wk_ref[...], T)
+
+    def turn(tokens):
+        q_turned = qc[0:tokens, :].astype(F32).T
+        k_turned = kc[0:tokens, :].astype(F32).T
+        qt[:, 0:tokens] = q_turned.astype(BF16)
+        kt[:, 0:tokens] = k_turned.astype(BF16)
+        uq[:, 0:tokens] = q_turned * (0.5 * use_prev[:, 0:tokens])
+        uk[:, 0:tokens] = k_turned * (0.5 * use_next[:, 0:tokens])
+
+    turn(T)
+    for c in loads[5:]:
+        c.wait()
+
+    def value_head(h, _):
+        cols = head_cols(h)
+        xv[h, 0:8, :] = jnp.zeros((8, HD), F32)
+        xv[h, 8:, :] = v_ref[:, cols].astype(F32)
+        vc[h] = conv(xv.at[h], wv_ref[:, cols], T)
+        return 0
+
+    lax.fori_loop(0, HEADS, value_head, 0)
 
     pl.semaphore_wait(barrier, len(greeted))
 
@@ -213,28 +287,9 @@
     inside = jnp.where(me > 0, 1.0, 0.0)
     xq[0:8, :] = halo_q[...].astype(F32)[8:16] * inside
     xk[0:8, :] = halo_k[...].astype(F32)[8:16] * inside
-    for h in range(HEADS):
-        xv[h, 0:8, :] = halo_v[:, h * HD : (h + 1) * HD].astype(F32)[8:16] * inside
-
-    def conv(x, w):
-        return w[0:1] * x[8 : 8 + T] + w[1:2] * x[7 : 7 + T] + w[2:3] * x[6 : 6 + T]
-
-    q = conv(xq, wq_ref[...]).astype(BF16)
-    k = conv(xk, wk_ref[...]).astype(BF16)
-    qc[...] = q
-    kc[...] = k
-    q_turned = q.astype(F32).T
-    k_turned = k.astype(F32).T
-    qt[...] = q_turned.astype(BF16)
-    kt[...] = k_turned.astype(BF16)
-    uq[...] = q_turned * (0.5 * use_prev)
-    uk[...] = k_turned * (0.5 * use_next)
-
-    def head_rows(h):
-        return pl.ds(pl.multiple_of(h * F, F), F)
-
-    def head_cols(h):
-        return pl.ds(pl.multiple_of(h * HD, HD), HD)
+    qc[0:16, :] = conv(xq, wq_ref[...], 16)
+    kc[0:16, :] = conv(xk, wk_ref[...], 16)
+    turn(128)
 
     def a_copy(tail, got, phase, h):
         return remote(
@@ -254,23 +309,22 @@
 
     def tail_head(h):
         cols = head_cols(h)
-        w = wv_ref[:, cols]
-        x = xv.at[h]
-        value = (
-            w[0:1] * x[8 : 8 + T, :] + w[1:2] * x[7 : 7 + T, :] + w[2:3] * x[6 : 6 + T, :]
-        ).astype(BF16)
-        vc[h] = value
+        xv[h, 0:8, :] = halo_v[:, cols].astype(F32)[8:16] * inside
+        vc[h, 0:16, :] = conv(xv.at[h], wv_ref[:, cols], 16)
+        value = vc[h]
         put_features(phik, h, uk[head_rows(h), :], use_next)
         tail1[h] = dot(phik[h], value, 1, 0).astype(BF16)
 
-    def tail_step(j, _):
-        h = (z + 1 + j) % ZN
+    def tail_step(h, _):
         tail_head(h)
-        a_copy(tail1, got1, 0, h).start()
+
+        @pl.when(h != z)
+        def _():
+            a_copy(tail1, got1, 0, h).start()
+
         return 0
 
-    lax.fori_loop(0, ZN - 1, tail_step, 0)
-    tail_head(z)
+    lax.fori_loop(0, HEADS, tail_step, 0)
     got1[z] = tail1[z]
 
     lane_head = lax.broadcasted_iota(jnp.int32, (1, HEADS * F), 1) // F
@@ -325,11 +379,8 @@
             send[i] = running.astype(BF16)
             running = got[i].astype(F32) + keeps[i] * running
 
-        def send_b(j, _):
-            b_copy(send, take, phase, (z + j) % ZN).start()
-            return 0
-
-        lax.fori_loop(1, ZN, send_b, 0)
+        for away in (4, 3, 5, 2, 6, 1, 7):
+            b_copy(send, take, phase, (z + away) % ZN).start()
         take[z] = send[z]
 
     scan(tail1, got1, tot1, ytot1, send1, inc, 0, False)
@@ -350,21 +401,25 @@
         tail2[h] = dot(phiq[h], grad, 1, 0).astype(BF16)
 
     local[...] = jnp.zeros(local.shape, F32)
-    forward_head(z)
+
+    def forward_step(h, _):
+        @pl.when(h != z)
+        def _():
+            b_arrival(send1, inc, 0, h).wait_recv()
+
+        forward_head(h)
+
+        @pl.when(h != z)
+        def _():
+            a_copy(tail2, got2, 1, h).start()
+
+        return 0
+
+    lax.fori_loop(0, HEADS, forward_step, 0)
     got2[z] = tail2[z]
 
-    def nearest(j):
-        away = (j + 1) // 2
-        return (z + ZN + away * (1 - 2 * (j % 2))) % ZN
-
-    def forward_step(j, _):
-        h = nearest(j)
-        b_arrival(send1, inc, 0, h).wait_recv()
-        forward_head(h)
-        a_copy(tail2, got2, 1, h).start()
-        return 0
-
-    lax.fori_loop(1, ZN, forward_step, 0)
+    store_mixed = pltpu.make_async_copy(mixed_ref, mixed_hbm, out_s.at[0])
+    store_mixed.start()
 
     def backward_step(h, _):
         grad = ga_ref[h]
@@ -397,15 +452,15 @@
                 g * xv[h, 8 - j : 8 - j + T, :], axis=0, keepdims=True
             )
 
-    last_head(z)
-
-    def last_step(j, _):
-        h = nearest(j)
-        b_arrival(send2, outg, 1, h).wait_recv()
+    def last_step(h, _):
+        @pl.when(h != z)
+        def _():
+            b_arrival(send2, outg, 1, h).wait_recv()
+
         last_head(h)
         return 0
 
-    lax.fori_loop(1, ZN, last_step, 0)
+    lax.fori_loop(0, HEADS, last_step, 0)
     gq = gqt[...].T
     gk = gkt[...].T
     gqs[0:T, :] = gq
@@ -428,15 +483,26 @@
         local[0, 4 + j : 5 + j, :] = jnp.sum(gq * xq[8 - j : 8 - j + T, :], axis=0, keepdims=True)
         local[1, 4 + j : 5 + j, :] = jnp.sum(gk * xk[8 - j : 8 - j + T, :], axis=0, keepdims=True)
 
-    def rz_copy(zz):
-        return remote(local.at[zz], red_z.at[z], rz_ss.at[zz], rz_rs.at[z], z_peer(zz))
-
-    def rz_arrival(zz):
-        return remote(local.at[zz], red_z.at[zz], rz_ss.at[zz], rz_rs.at[zz], z_peer(zz))
-
-    for j in range(1, ZN):
-        rz_copy((z + j) % ZN).start()
-    red_z[z] = local[z]
+    halves[0, 16:24, :] = local[0]
+    halves[1, 16:24, :] = local[1]
+    for h in range(HEADS):
+        halves[h // 4, 4 * (h % 4) : 4 * (h % 4) + 4, :] = local[h, 0:4, :]
+    to_core = remote(halves.at[1 - core], red_c, rc_ss.at[0], rc_rs.at[0], other)
+    to_core.start()
+    to_core.wait_recv()
+    mine = halves[core] + red_c[...]
+    one_xy[...] = mine
+    here = x * n_y + y
+    red_xy[here] = mine
+    to_plane = [
+        (
+            remote(one_xy, red_xy.at[here], rxy_ss.at[slot], rxy_rs.at[here], peer),
+            remote(one_xy, red_xy.at[slot], rxy_ss.at[slot], rxy_rs.at[slot], peer),
+        )
+        for slot, peer in plane
+    ]
+    for c, _ in to_plane:
+        c.start()
 
     for c in backs:
         c.wait_recv()
@@ -464,48 +530,33 @@
         return 0
 
     lax.fori_loop(0, HEADS, value_step, 0)
-
+    stores = [store_mixed]
+    for i, (src, dst) in enumerate([(gq_ref, gq_hbm), (gk_ref, gk_hbm), (gv_ref, gv_hbm)]):
+        stores.append(pltpu.make_async_copy(src, dst, out_s.at[1 + i]))
+        stores[-1].start()
+
+    for _, c in to_plane:
+        c.wait_recv()
+    mine = jnp.sum(red_xy[...], axis=0)
+    one_z[...] = mine
+    red_z[z] = mine
+
+    def rz(zz, slot):
+        return remote(one_z, red_z.at[slot], rz_ss.at[zz], rz_rs.at[slot], z_peer(zz))
+
+    for away in (4, 3, 5, 2, 6, 1, 7):
+        rz((z + away) % ZN, z).start()
     for j in range(1, ZN):
-        rz_arrival((z + j) % ZN).wait_recv()
-    tile = jnp.sum(red_z[...], axis=0)
-    one_y[...] = tile
-    red_y[y] = tile
-
-    def ry(yy, slot):
-        return remote(one_y, red_y.at[slot], ry_ss.at[yy], ry_rs.at[slot], y_peer(yy))
-
-    for j in range(1, n_y):
-        ry((y + j) % n_y, y).start()
-    for j in range(1, n_y):
-        ry((y + j) % n_y, (y + j) % n_y).wait_recv()
-    tile = jnp.sum(red_y[...], axis=0)
-    one_d[...] = tile
-    red_d[dp] = tile
-
-    def rd(dd, slot):
-        return remote(one_d, red_d.at[slot], rd_ss.at[dd], rd_rs.at[slot], {"dp": dd})
-
-    for j in range(1, n_dp):
-        rd((dp + j) % n_dp, dp).start()
-    for j in range(1, n_dp):
-        rd((dp + j) % n_dp, (dp + j) % n_dp).wait_recv()
-    tile = jnp.sum(red_d[...], axis=0)
-    one_z[...] = tile
-    all_z[z] = tile
-
-    def az(zz, slot):
-        return remote(one_z, all_z.at[slot], az_ss.at[zz], az_rs.at[slot], z_peer(zz))
-
-    for j in range(1, ZN):
-        az((z + j) % ZN, z).start()
-    for j in range(1, ZN):
-        az((z + j) % ZN, (z + j) % ZN).wait_recv()
-    gwq_ref[...] = all_z[0, 4:7, :]
-    gwk_ref[...] = all_z[1, 4:7, :]
-    for h in range(HEADS):
-        gwv_ref[:, h * HD : (h + 1) * HD] = all_z[h, 0:3, :]
-        gg_ref[:, h * HD : (h + 1) * HD] = all_z[h, 3:4, :]
-
+        rz((z + j) % ZN, (z + j) % ZN).wait_recv()
+    mine = jnp.sum(red_z[...], axis=0)
+    one_c[core] = mine
+    back_to_core = remote(one_c.at[core], one_c.at[core], ac_ss.at[0], ac_rs.at[0], other)
+    back_to_core.start()
+    remote(one_c.at[core], one_c.at[1 - core], ac_ss.at[0], ac_rs.at[0], other).wait_recv()
+    sums_ref[...] = one_c[...]
+
+    for c in stores:
+        c.wait()
     for c in halos:
         c.wait_send()
 
@@ -515,8 +566,7 @@
         a_copy(tail2, got2, 1, zz).wait_send()
         b_copy(send1, inc, 0, zz).wait_send()
         b_copy(send2, outg, 1, zz).wait_send()
-        rz_copy(zz).wait_send()
-        az(zz, z).wait_send()
+        rz(zz, z).wait_send()
         return 0
 
     lax.fori_loop(1, ZN, left, 0)
@@ -524,9 +574,40 @@
         yy = (y + j) % n_y
         remote(tot1, ytot1.at[y], y_ss.at[0, yy], y_rs.at[0, y], y_peer(yy)).wait_send()
         remote(tot2, ytot2.at[y], y_ss.at[1, yy], y_rs.at[1, y], y_peer(yy)).wait_send()
-        ry(yy, y).wait_send()
-    for j in range(1, n_dp):
-        rd((dp + j) % n_dp, dp).wait_send()
+    for c, _ in to_plane:
+        c.wait_send()
+    to_core.wait_send()
+    back_to_core.wait_send()
+
+
+def writer(mixed, gq, gk, gv, sums, mixed_o, gq_o, gk_o, gv_o, gwq_o, gwk_o, gwv_o, gg_o, gwq, gwk, gwv, gg, sems):
+    copies = [
+        pltpu.make_async_copy(src, dst, sems.at[i])
+        for i, (src, dst) in enumerate(
+            [
+                (mixed, mixed_o),
+                (gv, gv_o),
+                (gq, gq_o),
+                (gk, gk_o),
+                (gwq, gwq_o),
+                (gwk, gwk_o),
+                (gwv, gwv_o),
+                (gg, gg_o),
+            ]
+        )
+    ]
+    for c in copies[:4]:
+        c.start()
+    gwq[...] = sums[0, 20:23, :]
+    gwk[...] = sums[1, 20:23, :]
+    for h in range(HEADS):
+        base = 4 * (h % 4)
+        gwv[:, h * HD : (h + 1) * HD] = sums[h // 4, base : base + 3, :]
+        gg[:, h * HD : (h + 1) * HD] = sums[h // 4, base + 3 : base + 4, :]
+    for c in copies[4:]:
+        c.start()
+    for c in copies:
+        c.wait()
 
 
 def solution(mesh):
@@ -538,7 +619,22 @@
     def shards(q, k, v, wq, wk, wv, gain, lens, og):
         vmem = pl.BlockSpec(memory_space=pltpu.VMEM)
         state = (ROWS, HD)
+        hbm = pl.BlockSpec(memory_space=pltpu.HBM)
         scratch = [
+            pltpu.VMEM((T, wide), BF16),
+            pltpu.VMEM((T, thin), BF16),
+            pltpu.VMEM((T, thin), BF16),
+            pltpu.VMEM((T, wide), BF16),
+            pltpu.SemaphoreType.DMA((4,)),
+            pltpu.SMEM((1, DOCS), jnp.int32),
+            pltpu.VMEM((T, thin), BF16),
+            pltpu.VMEM((T, thin), BF16),
+            pltpu.VMEM((T, wide), BF16),
+            pltpu.VMEM((T, wide), BF16),
+            pltpu.VMEM((3, thin), F32),
+            pltpu.VMEM((3, thin), F32),
+            pltpu.VMEM((3, wide), F32),
+            pltpu.VMEM((1, wide), F32),
             pltpu.VMEM((T + 8, thin), F32),
             pltpu.VMEM((T + 8, thin), F32),
             pltpu.VMEM((HEADS, T + 8, HD), F32),
@@ -578,22 +674,38 @@
                 pltpu.VMEM((ZN,) + state, BF16),
                 pltpu.VMEM((HEADS,) + state, BF16),
             ]
-        tile = (8, HD)
+        half = (24, HD)
         scratch += [
-            pltpu.VMEM(tile, F32),
-            pltpu.VMEM((ZN,) + tile, F32),
-            pltpu.VMEM(tile, F32),
-            pltpu.VMEM((n_y,) + tile, F32),
-            pltpu.VMEM(tile, F32),
-            pltpu.VMEM((n_dp,) + tile, F32),
-            pltpu.VMEM(tile, F32),
-            pltpu.VMEM((ZN,) + tile, F32),
+            pltpu.VMEM((2,) + half, F32),
+            pltpu.VMEM(half, F32),
+            pltpu.VMEM((n_dp // 2 * n_y,) + half, F32),
+            pltpu.VMEM(half, F32),
+            pltpu.VMEM((ZN,) + half, F32),
+            pltpu.VMEM(half, F32),
+            pltpu.VMEM((2,) + half, F32),
+            pltpu.SemaphoreType.DMA((9,)),
         ]
         dma = pltpu.SemaphoreType.DMA
-        for counts in ((3,), (3,), (2, ZN), (2, n_y), (2, ZN), (ZN,), (n_y,), (n_dp,), (ZN,)):
+        for counts in ((3,), (3,), (2, ZN), (2, n_y), (2, ZN), (1,), (n_dp // 2 * n_y,), (ZN,), (1,)):
             scratch += [dma(counts), dma(counts)]
         outs = pl.pallas_call(
             functools.partial(kernel, n_dp, n_ctx),
+            out_shape=(
+                jax.ShapeDtypeStruct((T, wide), BF16),
+                jax.ShapeDtypeStruct((T, thin), BF16),
+                jax.ShapeDtypeStruct((T, thin), BF16),
+                jax.ShapeDtypeStruct((T, wide), BF16),
+                jax.ShapeDtypeStruct((2,) + half, F32),
+            ),
+            in_specs=[hbm] * 9,
+            out_specs=(hbm,) * 4 + (vmem,),
+            scratch_shapes=scratch,
+            compiler_params=pltpu.CompilerParams(
+                collective_id=0, has_side_effects=True, vmem_limit_bytes=64 * 2**20 - 2**18
+            ),
+        )(lens, q[0], k[0], v[0], og[0], wq, wk, wv, gain[None])
+        outs = pl.pallas_call(
+            writer,
             out_shape=(
                 jax.ShapeDtypeStruct((T, wide), BF16),
                 jax.ShapeDtypeStruct((T, thin), BF16),
@@ -604,13 +716,16 @@
                 jax.ShapeDtypeStruct((3, wide), F32),
                 jax.ShapeDtypeStruct((1, wide), F32),
             ),
-            in_specs=[pl.BlockSpec(memory_space=pltpu.SMEM)] + [vmem] * 8,
-            out_specs=(vmem,) * 8,
-            scratch_shapes=scratch,
-            compiler_params=pltpu.CompilerParams(
-                collective_id=0, has_side_effects=True, vmem_limit_bytes=48 * 2**20
-            ),
-        )(lens, q[0], k[0], v[0], og[0], wq, wk, wv, gain[None])
+            in_specs=[hbm] * 4 + [vmem],
+            out_specs=(hbm,) * 8,
+            scratch_shapes=[
+                pltpu.VMEM((3, thin), F32),
+                pltpu.VMEM((3, thin), F32),
+                pltpu.VMEM((3, wide), F32),
+                pltpu.VMEM((1, wide), F32),
+                pltpu.SemaphoreType.DMA((8,)),
+            ],
+        )(*outs)
         mixed, gq, gk, gv, gwq, gwk, gwv, gg = outs
         return mixed[None], gq[None], gk[None], gv[None], gwq, gwk, gwv, gg[0]
 

time: 87.1 us -> 111 us (1.27)
  Pallas kernels: 75.7 us -> 110 us
  local copies, waits for them, and re-layouts: 10.4 us -> 0 us
    pallas_call x0 -> x1, Pallas kernels: none -> 37.7 us  [shards(): pl.pallas_call(writer, out_shape=(jax.ShapeDtypeStruct((T, wide), BF16),...]
    unnamed x26 -> x0, local copies, waits for them, and re-layouts: 10.4 us -> none
    pallas_call x1, Pallas kernels: 75.7 us -> 72.3 us  [shards(): pl.pallas_call(functools.partial(kernel, n_dp, n_ctx), out_shape=(jax.Sha...]
where the time goes in v2:
time: 111 us
  Pallas kernels  110 us (99%)
    pallas_call x1, Pallas kernels, shards(): pl.pallas_call(functools.partial(kernel, n_dp, n_ctx), out_shape=(jax.Sha...  72.3 us
    pallas_call x1, Pallas kernels, shards(): pl.pallas_call(writer, out_shape=(jax.ShapeDtypeStruct((T, wide), BF16),...  37.7 us

profile of v2, /device:TPU:1, one launch (start us, length us, event | category | flops | bytes accessed | tf_op | source)
XLA Modules:
  0.0 110.6 jit_solution(2957656561536757133)
XLA Ops:
  0.6 72.3 %shard_map.152 = (bf16[256,1024]{1,0:T(8,128)(2,1)}, bf16[256,128]{1,0:T(8,128)(2,1)}, bf16[256,128]{1,0:T(8,128)(2,1)}, bf16[256,1024]{1,0:T(8,128)(2,1)}, f32[2,24,128]{2,1,0:T(8,128)}) custom-call(s32[1,8]{1,0:T(1,128)} %lens_hbm.1, bf16[256,128]{1,0:T(8,128)(2,1)} %bitcast.12, bf16[256,128]{1,0:T(8,128)(2,1)} %bitcast.13, bf16[256,1024]{1,0:T(8,128)(2,1)} %bitcast.10, ...), custom_call_target="tpu_custom_call" | custom-call | tf_op jit(solution)/shard_map/pallas_call | solution.py:691
  73.0 37.7 %shard_map.153 = (bf16[256,1024]{1,0:T(8,128)(2,1)}, bf16[256,128]{1,0:T(8,128)(2,1)}, bf16[256,128]{1,0:T(8,128)(2,1)}, bf16[256,1024]{1,0:T(8,128)(2,1)}, f32[...) custom-call(bf16[256,1024]{1,0:T(8,128)(2,1)} %get-tuple-element.21.mixed, ...), custom_call_target="tpu_custom_call" | custom-call | tf_op jit(solution)/shard_map/pallas_call | solution.py:707

commit v3 on v2

--- a/solution.py
+++ b/solution.py
@@ -580,33 +580,47 @@
     back_to_core.wait_send()
 
 
-def writer(mixed, gq, gk, gv, sums, mixed_o, gq_o, gk_o, gv_o, gwq_o, gwk_o, gwv_o, gg_o, gwq, gwk, gwv, gg, sems):
-    copies = [
-        pltpu.make_async_copy(src, dst, sems.at[i])
+def writer(*refs):
+    mixed, gq, gk, gv, sums_hbm = refs[:5]
+    outs = refs[5:13]
+    held = refs[13:17]
+    sums, gwq, gwk, gwv, gg, in_s, out_s = refs[17:]
+    ins = [
+        pltpu.make_async_copy(src, dst, in_s.at[i])
+        for i, (src, dst) in enumerate(
+            [(sums_hbm, sums), (mixed, held[0]), (gv, held[3]), (gq, held[1]), (gk, held[2])]
+        )
+    ]
+    stores = [
+        pltpu.make_async_copy(src, dst, out_s.at[i])
         for i, (src, dst) in enumerate(
             [
-                (mixed, mixed_o),
-                (gv, gv_o),
-                (gq, gq_o),
-                (gk, gk_o),
-                (gwq, gwq_o),
-                (gwk, gwk_o),
-                (gwv, gwv_o),
-                (gg, gg_o),
+                (held[0], outs[0]),
+                (held[3], outs[3]),
+                (held[1], outs[1]),
+                (held[2], outs[2]),
+                (gwq, outs[4]),
+                (gwk, outs[5]),
+                (gwv, outs[6]),
+                (gg, outs[7]),
             ]
         )
     ]
-    for c in copies[:4]:
+    for c in ins:
         c.start()
+    for i in (1, 2, 3, 4):
+        ins[i].wait()
+        stores[i - 1].start()
+    ins[0].wait()
     gwq[...] = sums[0, 20:23, :]
     gwk[...] = sums[1, 20:23, :]
     for h in range(HEADS):
         base = 4 * (h % 4)
         gwv[:, h * HD : (h + 1) * HD] = sums[h // 4, base : base + 3, :]
         gg[:, h * HD : (h + 1) * HD] = sums[h // 4, base + 3 : base + 4, :]
-    for c in copies[4:]:
+    for c in stores[4:]:
         c.start()
-    for c in copies:
+    for c in stores:
         c.wait()
 
 
@@ -716,13 +730,19 @@
                 jax.ShapeDtypeStruct((3, wide), F32),
                 jax.ShapeDtypeStruct((1, wide), F32),
             ),
-            in_specs=[hbm] * 4 + [vmem],
+            in_specs=[hbm] * 5,
             out_specs=(hbm,) * 8,
             scratch_shapes=[
+                pltpu.VMEM((T, wide), BF16),
+                pltpu.VMEM((T, thin), BF16),
+                pltpu.VMEM((T, thin), BF16),
+                pltpu.VMEM((T, wide), BF16),
+                pltpu.VMEM((2,) + half, F32),
                 pltpu.VMEM((3, thin), F32),
                 pltpu.VMEM((3, thin), F32),
                 pltpu.VMEM((3, wide), F32),
                 pltpu.VMEM((1, wide), F32),
+                pltpu.SemaphoreType.DMA((5,)),
                 pltpu.SemaphoreType.DMA((8,)),
             ],
         )(*outs)

time: 111 us -> 75.3 us (0.68)
  Pallas kernels: 110 us -> 74.5 us
    pallas_call x1, Pallas kernels: 37.7 us -> 2.18 us  [shards(): pl.pallas_call(writer, out_shape=(jax.ShapeDtypeStruct((T, wide), BF16),...]
where the time goes in v3:
time: 75.3 us; the launch traced here: 75.1 us
  Pallas kernels  74.5 us (99%)
    pallas_call x1, Pallas kernels, shards(): pl.pallas_call(functools.partial(kernel, n_dp, n_ctx), out_shape=(jax.Sha...  72.3 us
    pallas_call x1, Pallas kernels, shards(): pl.pallas_call(writer, out_shape=(jax.ShapeDtypeStruct((T, wide), BF16),...  2.18 us

profile of v3, /device:TPU:1, one launch (start us, length us, event | category | flops | bytes accessed | tf_op | source)
XLA Modules:
  0.0 75.1 jit_solution(16848074365921573422)
XLA Ops:
  0.6 72.3 %shard_map.152 = (bf16[256,1024]{1,0:T(8,128)(2,1)}, bf16[256,128]{1,0:T(8,128)(2,1)}, bf16[256,128]{1,0:T(8,128)(2,1)}, bf16[256,1024]{1,0:T(8,128)(2,1)}, f32[2,24,128]{2,1,0:T(8,128)}) custom-call(s32[1,8]{1,0:T(1,128)} %lens_hbm.1, bf16[256,128]{1,0:T(8,128)(2,1)} %bitcast.12, bf16[256,128]{1,0:T(8,128)(2,1)} %bitcast.13, bf16[256,1024]{1,0:T(8,128)(2,1)} %bitcast.10, ...), custom_call_target="tpu_custom_call" | custom-call | tf_op jit(solution)/shard_map/pallas_call | solution.py:705
  73.0 2.2 %shard_map.153 = (bf16[256,1024]{1,0:T(8,128)(2,1)}, bf16[256,128]{1,0:T(8,128)(2,1)}, bf16[256,128]{1,0:T(8,128)(2,1)}, bf16[256,1024]{1,0:T(8,128)(2,1)}, f32[...) custom-call(bf16[256,1024]{1,0:T(8,128)(2,1)} %get-tuple-element.21.refs_0_, ...), custom_call_target="tpu_custom_call" | custom-call | tf_op jit(solution)/shard_map/pallas_call | solution.py:721

commit v4 on v3

--- a/solution.py
+++ b/solution.py
@@ -13,6 +13,8 @@
 T = 256
 DOCS = 8
 ROWS = 160
+PART = ROWS // 2
+GROUP = HEADS // 2
 ZN = 8
 EPS = 1e-06
 MESH = pl.DeviceIdType.MESH
@@ -291,21 +293,58 @@
     kc[0:16, :] = conv(xk, wk_ref[...], 16)
     turn(128)
 
-    def a_copy(tail, got, phase, h):
+    def owned(zz):
+        return pl.ds(pl.multiple_of(PART * (zz % 2), 16), PART)
+
+    def a_copy(tail, got, phase, g, zz):
         return remote(
-            tail.at[h], got.at[z], a_ss.at[phase, h], a_rs.at[phase, z], z_peer(h)
-        )
-
-    def a_arrival(tail, got, phase, zz):
+            tail.at[GROUP * g + zz // 2, owned(zz), :],
+            got.at[g, z],
+            a_ss.at[phase, g, zz],
+            a_rs.at[phase, g, z],
+            z_peer(zz),
+        )
+
+    def a_arrival(tail, got, phase, g, zz):
         return remote(
-            tail.at[zz], got.at[zz], a_ss.at[phase, zz], a_rs.at[phase, zz], z_peer(zz)
-        )
-
-    def b_copy(send, take, phase, zz):
-        return remote(send.at[zz], take.at[z], b_ss.at[phase, zz], b_rs.at[phase, z], z_peer(zz))
-
-    def b_arrival(send, take, phase, h):
-        return remote(send.at[h], take.at[h], b_ss.at[phase, h], b_rs.at[phase, h], z_peer(h))
+            tail.at[GROUP * g + zz // 2, owned(zz), :],
+            got.at[g, zz],
+            a_ss.at[phase, g, zz],
+            a_rs.at[phase, g, zz],
+            z_peer(zz),
+        )
+
+    def b_copy(send, take, phase, g, zz):
+        return remote(
+            send.at[g, zz],
+            take.at[GROUP * g + z // 2, owned(z), :],
+            b_ss.at[phase, g, zz],
+            b_rs.at[phase, g, z],
+            z_peer(zz),
+        )
+
+    def b_arrival(send, take, phase, g, zz):
+        return remote(
+            send.at[g, zz],
+            take.at[GROUP * g + zz // 2, owned(zz), :],
+            b_ss.at[phase, g, zz],
+            b_rs.at[phase, g, zz],
+            z_peer(zz),
+        )
+
+    def send_tail(tail, got, phase, g, p):
+        for zz in (2 * p, 2 * p + 1):
+
+            @pl.when(zz != z)
+            def _():
+                a_copy(tail, got, phase, g, zz).start()
+
+    def wait_state(send, take, phase, g, p):
+        for zz in (2 * p, 2 * p + 1):
+
+            @pl.when(zz != z)
+            def _():
+                b_arrival(send, take, phase, g, zz).wait_recv()
 
     def tail_head(h):
         cols = head_cols(h)
@@ -315,17 +354,15 @@
         put_features(phik, h, uk[head_rows(h), :], use_next)
         tail1[h] = dot(phik[h], value, 1, 0).astype(BF16)
 
-    def tail_step(h, _):
-        tail_head(h)
-
-        @pl.when(h != z)
-        def _():
-            a_copy(tail1, got1, 0, h).start()
-
-        return 0
-
-    lax.fori_loop(0, HEADS, tail_step, 0)
-    got1[z] = tail1[z]
+    for g in range(2):
+
+        def tail_step(i, _, g=g):
+            p = (z // 2 + 2 + i) % GROUP
+            tail_head(GROUP * g + p)
+            send_tail(tail1, got1, 0, g, p)
+            return 0
+
+        lax.fori_loop(0, GROUP, tail_step, 0)
 
     lane_head = lax.broadcasted_iota(jnp.int32, (1, HEADS * F), 1) // F
 
@@ -343,45 +380,52 @@
     lax.fori_loop(0, HEADS, inner_step, 0)
 
     def scan(tail, got, tot, ytot, send, take, phase, reverse):
-        def wait_a(j, _):
-            a_arrival(tail, got, phase, (z + j) % ZN).wait_recv()
-            return 0
-
-        lax.fori_loop(1, ZN, wait_a, 0)
         order = range(ZN - 1, -1, -1) if reverse else range(ZN)
-        running = jnp.zeros((ROWS, HD), F32)
-        keeps = {}
-        for i in order:
-            keeps[i] = keep_of(y * ZN + i)
-            running = got[i].astype(F32) + keeps[i] * running
-        tot[...] = running.astype(BF16)
-        ytot[y] = running.astype(BF16)
-
-        def y_copy(j):
+        keeps = [keep_of(y * ZN + i) for i in range(ZN)]
+
+        def y_copy(g, j):
             yy = (y + j) % n_y
-            return remote(tot, ytot.at[y], y_ss.at[phase, yy], y_rs.at[phase, y], y_peer(yy))
-
-        def y_arrival(j):
+            return remote(
+                tot.at[g], ytot.at[g, y], y_ss.at[phase, g, yy], y_rs.at[phase, g, y], y_peer(yy)
+            )
+
+        def y_arrival(g, j):
             yy = (y + j) % n_y
-            return remote(tot, ytot.at[yy], y_ss.at[phase, yy], y_rs.at[phase, yy], y_peer(yy))
-
-        for j in range(1, n_y):
-            y_copy(j).start()
-        for j in range(1, n_y):
-            y_arrival(j).wait_recv()
-        carry = jnp.zeros((ROWS, HD), F32)
-        for g in range(n_y - 1, 0, -1) if reverse else range(n_y - 1):
-            counts = jnp.where(g > y if reverse else g < y, 1.0, 0.0)
-            onward = ytot[g].astype(F32) + keep_group(g) * carry
-            carry = counts * onward + (1.0 - counts) * carry
-        running = carry
-        for i in order:
-            send[i] = running.astype(BF16)
-            running = got[i].astype(F32) + keeps[i] * running
-
-        for away in (4, 3, 5, 2, 6, 1, 7):
-            b_copy(send, take, phase, (z + away) % ZN).start()
-        take[z] = send[z]
+            return remote(
+                tot.at[g], ytot.at[g, yy], y_ss.at[phase, g, yy], y_rs.at[phase, g, yy], y_peer(yy)
+            )
+
+        for g in range(2):
+            got[g, z] = tail[GROUP * g + z // 2, owned(z), :]
+
+            def wait_a(j, _, g=g):
+                a_arrival(tail, got, phase, g, (z + j) % ZN).wait_recv()
+                return 0
+
+            lax.fori_loop(1, ZN, wait_a, 0)
+            running = jnp.zeros((PART, HD), F32)
+            for i in order:
+                running = got[g, i].astype(F32) + keeps[i] * running
+            total = running.astype(BF16)
+            tot[g] = total
+            ytot[g, y] = total
+            for j in range(1, n_y):
+                y_copy(g, j).start()
+        for g in range(2):
+            for j in range(1, n_y):
+                y_arrival(g, j).wait_recv()
+            carry = jnp.zeros((PART, HD), F32)
+            for r in range(n_y - 1, 0, -1) if reverse else range(n_y - 1):
+                counts = jnp.where(r > y if reverse else r < y, 1.0, 0.0)
+                onward = ytot[g, r].astype(F32) + keep_group(r) * carry
+                carry = counts * onward + (1.0 - counts) * carry
+            running = carry
+            for i in order:
+                send[g, i] = running.astype(BF16)
+                running = got[g, i].astype(F32) + keeps[i] * running
+            for away in (4, 3, 5, 2, 6, 1, 7):
+                b_copy(send, take, phase, g, (z + away) % ZN).start()
+            take[GROUP * g + z // 2, owned(z), :] = send[g, z]
 
     scan(tail1, got1, tot1, ytot1, send1, inc, 0, False)
 
@@ -402,21 +446,16 @@
 
     local[...] = jnp.zeros(local.shape, F32)
 
-    def forward_step(h, _):
-        @pl.when(h != z)
-        def _():
-            b_arrival(send1, inc, 0, h).wait_recv()
-
-        forward_head(h)
-
-        @pl.when(h != z)
-        def _():
-            a_copy(tail2, got2, 1, h).start()
-
-        return 0
-
-    lax.fori_loop(0, HEADS, forward_step, 0)
-    got2[z] = tail2[z]
+    for g in range(2):
+
+        def forward_step(i, _, g=g):
+            p = (z // 2 + 1 + i) % GROUP
+            wait_state(send1, inc, 0, g, p)
+            forward_head(GROUP * g + p)
+            send_tail(tail2, got2, 1, g, p)
+            return 0
+
+        lax.fori_loop(0, GROUP, forward_step, 0)
 
     store_mixed = pltpu.make_async_copy(mixed_ref, mixed_hbm, out_s.at[0])
     store_mixed.start()
@@ -452,15 +491,15 @@
                 g * xv[h, 8 - j : 8 - j + T, :], axis=0, keepdims=True
             )
 
-    def last_step(h, _):
-        @pl.when(h != z)
-        def _():
-            b_arrival(send2, outg, 1, h).wait_recv()
-
-        last_head(h)
-        return 0
-
-    lax.fori_loop(0, HEADS, last_step, 0)
+    for g in range(2):
+
+        def last_step(i, _, g=g):
+            p = (z // 2 + 1 + i) % GROUP
+            wait_state(send2, outg, 1, g, p)
+            last_head(GROUP * g + p)
+            return 0
+
+        lax.fori_loop(0, GROUP, last_step, 0)
     gq = gqt[...].T
     gk = gkt[...].T
     gqs[0:T, :] = gq
@@ -562,18 +601,22 @@
 
     def left(j, _):
         zz = (z + j) % ZN
-        a_copy(tail1, got1, 0, zz).wait_send()
-        a_copy(tail2, got2, 1, zz).wait_send()
-        b_copy(send1, inc, 0, zz).wait_send()
-        b_copy(send2, outg, 1, zz).wait_send()
+        for g in range(2):
+            a_copy(tail1, got1, 0, g, zz).wait_send()
+            a_copy(tail2, got2, 1, g, zz).wait_send()
+            b_copy(send1, inc, 0, g, zz).wait_send()
+            b_copy(send2, outg, 1, g, zz).wait_send()
         rz(zz, z).wait_send()
         return 0
 
     lax.fori_loop(1, ZN, left, 0)
     for j in range(1, n_y):
         yy = (y + j) % n_y
-        remote(tot1, ytot1.at[y], y_ss.at[0, yy], y_rs.at[0, y], y_peer(yy)).wait_send()
-        remote(tot2, ytot2.at[y], y_ss.at[1, yy], y_rs.at[1, y], y_peer(yy)).wait_send()
+        for g in range(2):
+            for phase, tot, ytot in ((0, tot1, ytot1), (1, tot2, ytot2)):
+                remote(
+                    tot.at[g], ytot.at[g, y], y_ss.at[phase, g, yy], y_rs.at[phase, g, y], y_peer(yy)
+                ).wait_send()
     for c, _ in to_plane:
         c.wait_send()
     to_core.wait_send()
@@ -682,10 +725,10 @@
         for _ in range(2):
             scratch += [
                 pltpu.VMEM((HEADS,) + state, BF16),
-                pltpu.VMEM((ZN,) + state, BF16),
-                pltpu.VMEM(state, BF16),
-                pltpu.VMEM((n_y,) + state, BF16),
-                pltpu.VMEM((ZN,) + state, BF16),
+                pltpu.VMEM((2, ZN, PART, HD), BF16),
+                pltpu.VMEM((2, PART, HD), BF16),
+                pltpu.VMEM((2, n_y, PART, HD), BF16),
+                pltpu.VMEM((2, ZN, PART, HD), BF16),
                 pltpu.VMEM((HEADS,) + state, BF16),
             ]
         half = (24, HD)
@@ -700,7 +743,7 @@
             pltpu.SemaphoreType.DMA((9,)),
         ]
         dma = pltpu.SemaphoreType.DMA
-        for counts in ((3,), (3,), (2, ZN), (2, n_y), (2, ZN), (1,), (n_dp // 2 * n_y,), (ZN,), (1,)):
+        for counts in ((3,), (3,), (2, 2, ZN), (2, 2, n_y), (2, 2, ZN), (1,), (n_dp // 2 * n_y,), (ZN,), (1,)):
             scratch += [dma(counts), dma(counts)]
         outs = pl.pallas_call(
             functools.partial(kernel, n_dp, n_ctx),

time: 75.3 us -> 71.2 us (0.946)
  Pallas kernels: 74.5 us -> 70.4 us
    pallas_call x1, Pallas kernels: 72.3 us -> 68.3 us  [shards(): pl.pallas_call(functools.partial(kernel, n_dp, n_ctx), out_shape=(jax.Sha...]
where the time goes in v4:
time: 71.2 us; the launch traced here: 71.1 us
  Pallas kernels  70.4 us (99%)
    pallas_call x1, Pallas kernels, shards(): pl.pallas_call(functools.partial(kernel, n_dp, n_ctx), out_shape=(jax.Sha...  68.3 us
    pallas_call x1, Pallas kernels, shards(): pl.pallas_call(writer, out_shape=(jax.ShapeDtypeStruct((T, wide), BF16),...  2.18 us

profile of v4, /device:TPU:1, one launch (start us, length us, event | category | flops | bytes accessed | tf_op | source)
XLA Modules:
  0.0 71.1 jit_solution(5038601456886055752)
XLA Ops:
  0.6 68.3 %shard_map.152 = (bf16[256,1024]{1,0:T(8,128)(2,1)}, bf16[256,128]{1,0:T(8,128)(2,1)}, bf16[256,128]{1,0:T(8,128)(2,1)}, bf16[256,1024]{1,0:T(8,128)(2,1)}, f32[2,24,128]{2,1,0:T(8,128)}) custom-call(s32[1,8]{1,0:T(1,128)} %lens_hbm.1, bf16[256,128]{1,0:T(8,128)(2,1)} %bitcast.12, bf16[256,128]{1,0:T(8,128)(2,1)} %bitcast.13, bf16[256,1024]{1,0:T(8,128)(2,1)} %bitcast.10, ...), custom_call_target="tpu_custom_call" | custom-call | tf_op jit(solution)/shard_map/pallas_call | solution.py:748
  68.9 2.2 %shard_map.153 = (bf16[256,1024]{1,0:T(8,128)(2,1)}, bf16[256,128]{1,0:T(8,128)(2,1)}, bf16[256,128]{1,0:T(8,128)(2,1)}, bf16[256,1024]{1,0:T(8,128)(2,1)}, f32[...) custom-call(bf16[256,1024]{1,0:T(8,128)(2,1)} %get-tuple-element.21.refs_0_, ...), custom_call_target="tpu_custom_call" | custom-call | tf_op jit(solution)/shard_map/pallas_call | solution.py:764

commit v5 on v4

--- a/solution.py
+++ b/solution.py
@@ -31,12 +31,13 @@
 
 
 def put_features(out, h, u, ones):
-    out[h, 0:16, :] = (u * u * (0.5**0.5)).astype(BF16)
+    n = u.shape[1]
+    out[h, 0:16, 0:n] = (u * u * (0.5**0.5)).astype(BF16)
     for d in range(1, 8):
-        out[h, 16 * d : 16 * d + 16, :] = (u * turned(u, d)).astype(BF16)
-    out[h, 128:144, :] = u.astype(BF16)
-    rest = jnp.where(lax.broadcasted_iota(jnp.int32, (8, T), 0) == 0, ones, 0.0)
-    out[h, 144:160, :] = jnp.concatenate([u[0:8] * u[8:16], rest], axis=0).astype(BF16)
+        out[h, 16 * d : 16 * d + 16, 0:n] = (u * turned(u, d)).astype(BF16)
+    out[h, 128:144, 0:n] = u.astype(BF16)
+    rest = jnp.where(lax.broadcasted_iota(jnp.int32, (8, n), 0) == 0, ones, 0.0)
+    out[h, 144:160, 0:n] = jnp.concatenate([u[0:8] * u[8:16], rest], axis=0).astype(BF16)
 
 
 def pull_features(g, u, ones):
@@ -103,12 +104,10 @@
     gqs,
     gks,
     local,
-    halo_q,
-    halo_k,
-    halo_v,
-    back_q,
-    back_k,
-    back_v,
+    rim,
+    rim_got,
+    back_rim,
+    back_got,
     tail1,
     got1,
     tot1,
@@ -238,10 +237,10 @@
         ).astype(BF16)
 
     def head_rows(h):
-        return pl.ds(pl.multiple_of(h * F, F), F)
+        return pl.ds(h * F if isinstance(h, int) else pl.multiple_of(h * F, F), F)
 
     def head_cols(h):
-        return pl.ds(pl.multiple_of(h * HD, HD), HD)
+        return pl.ds(h * HD if isinstance(h, int) else pl.multiple_of(h * HD, HD), HD)
 
     xq[0:8, :] = jnp.zeros((8, HEADS * F), F32)
     xk[0:8, :] = jnp.zeros((8, HEADS * F), F32)
@@ -269,7 +268,8 @@
         vc[h] = conv(xv.at[h], wv_ref[:, cols], T)
         return 0
 
-    lax.fori_loop(0, HEADS, value_head, 0)
+    for h in range(HEADS):
+        value_head(h, 0)
 
     pl.semaphore_wait(barrier, len(greeted))
 
@@ -278,17 +278,24 @@
             src_ref=src, dst_ref=dst, send_sem=ss, recv_sem=rs, device_id=peer, device_id_type=MESH
         )
 
-    halos = [
-        remote(ref.at[T - 16 :, :], dst, halo_ss.at[i], halo_rs.at[i], {"ctx": after})
-        for i, (ref, dst) in enumerate([(q_ref, halo_q), (k_ref, halo_k), (v_ref, halo_v)])
-    ]
-    for c in halos:
-        c.start()
-    for c in halos:
-        c.wait_recv()
+    rim[16:24, :] = jnp.zeros((8, HD), F32)
+    for j in range(2):
+        row = T + 6 + j
+        for h in range(HEADS):
+            rim[8 * j + h : 8 * j + h + 1, :] = xv[h, row : row + 1, :]
+        rim[16 + j : 17 + j, :] = xq[row : row + 1, :]
+        rim[18 + j : 19 + j, :] = xk[row : row + 1, :]
+    halo = remote(rim, rim_got, halo_ss.at[0], halo_rs.at[0], {"ctx": after})
+    halo.start()
+    for h in range(HEADS):
+        put_features(phik, h, uk[head_rows(h), :], use_next)
+    halo.wait_recv()
     inside = jnp.where(me > 0, 1.0, 0.0)
-    xq[0:8, :] = halo_q[...].astype(F32)[8:16] * inside
-    xk[0:8, :] = halo_k[...].astype(F32)[8:16] * inside
+    for j in range(2):
+        for h in range(HEADS):
+            xv[h, 6 + j : 7 + j, :] = rim_got[8 * j + h : 8 * j + h + 1, :] * inside
+        xq[6 + j : 7 + j, :] = rim_got[16 + j : 17 + j, :] * inside
+        xk[6 + j : 7 + j, :] = rim_got[18 + j : 19 + j, :] * inside
     qc[0:16, :] = conv(xq, wq_ref[...], 16)
     kc[0:16, :] = conv(xk, wk_ref[...], 16)
     turn(128)
@@ -348,10 +355,9 @@
 
     def tail_head(h):
         cols = head_cols(h)
-        xv[h, 0:8, :] = halo_v[:, cols].astype(F32)[8:16] * inside
         vc[h, 0:16, :] = conv(xv.at[h], wv_ref[:, cols], 16)
         value = vc[h]
-        put_features(phik, h, uk[head_rows(h), :], use_next)
+        put_features(phik, h, uk[head_rows(h), 0:128], use_next[:, 0:128])
         tail1[h] = dot(phik[h], value, 1, 0).astype(BF16)
 
     for g in range(2):
@@ -377,7 +383,8 @@
         put_features(phiq, h, uq[head_rows(h), :], use_prev)
         return 0
 
-    lax.fori_loop(0, HEADS, inner_step, 0)
+    for h in range(HEADS):
+        inner_step(h, 0)
 
     def scan(tail, got, tot, ytot, send, take, phase, reverse):
         order = range(ZN - 1, -1, -1) if reverse else range(ZN)
@@ -472,7 +479,8 @@
         gvs[h, 0:T, :] = dot(kern[h], grad, 0, 0)
         return 0
 
-    lax.fori_loop(0, HEADS, backward_step, 0)
+    for h in range(HEADS):
+        backward_step(h, 0)
 
     scan(tail2, got2, tot2, ytot2, send2, outg, 1, True)
 
@@ -505,18 +513,14 @@
     gqs[0:T, :] = gq
     gks[0:T, :] = gk
 
-    backs = [
-        remote(src, dst, back_ss.at[i], back_rs.at[i], {"ctx": before})
-        for i, (src, dst) in enumerate(
-            [
-                (gqs.at[0:8, :], back_q),
-                (gks.at[0:8, :], back_k),
-                (gvs.at[:, 0:8, :], back_v),
-            ]
-        )
-    ]
-    for c in backs:
-        c.start()
+    back_rim[16:24, :] = jnp.zeros((8, HD), F32)
+    for j in range(2):
+        for h in range(HEADS):
+            back_rim[8 * j + h : 8 * j + h + 1, :] = gvs[h, j : j + 1, :]
+        back_rim[16 + j : 17 + j, :] = gqs[j : j + 1, :]
+        back_rim[18 + j : 19 + j, :] = gks[j : j + 1, :]
+    back = remote(back_rim, back_got, back_ss.at[0], back_rs.at[0], {"ctx": before})
+    back.start()
 
     for j in range(3):
         local[0, 4 + j : 5 + j, :] = jnp.sum(gq * xq[8 - j : 8 - j + T, :], axis=0, keepdims=True)
@@ -543,14 +547,25 @@
     for c, _ in to_plane:
         c.start()
 
-    for c in backs:
+    for _, c in to_plane:
         c.wait_recv()
+    mine = jnp.sum(red_xy[...], axis=0)
+    one_z[...] = mine
+    red_z[z] = mine
+
+    def rz(zz, slot):
+        return remote(one_z, red_z.at[slot], rz_ss.at[zz], rz_rs.at[slot], z_peer(zz))
+
+    for away in (4, 3, 5, 2, 6, 1, 7):
+        rz((z + away) % ZN, z).start()
+    back.wait_recv()
     inside_next = jnp.where(me < n_ctx - 1, 1.0, 0.0)
-    gqs[T : T + 8, :] = back_q[...] * inside_next
-    gks[T : T + 8, :] = back_k[...] * inside_next
-    for c in backs:
-        c.wait_send()
-    gvs[:, T : T + 8, :] = back_v[...] * inside_next
+    for j in range(2):
+        row = T + j
+        for h in range(HEADS):
+            gvs[h, row : row + 1, :] = back_got[8 * j + h : 8 * j + h + 1, :] * inside_next
+        gqs[row : row + 1, :] = back_got[16 + j : 17 + j, :] * inside_next
+        gks[row : row + 1, :] = back_got[18 + j : 19 + j, :] * inside_next
 
     def conv_back(g, w):
         return (w[0:1] * g[0:T] + w[1:2] * g[1 : 1 + T] + w[2:3] * g[2 : 2 + T]).astype(BF16)
@@ -568,23 +583,13 @@
         ).astype(BF16)
         return 0
 
-    lax.fori_loop(0, HEADS, value_step, 0)
+    for h in range(HEADS):
+        value_step(h, 0)
     stores = [store_mixed]
     for i, (src, dst) in enumerate([(gq_ref, gq_hbm), (gk_ref, gk_hbm), (gv_ref, gv_hbm)]):
         stores.append(pltpu.make_async_copy(src, dst, out_s.at[1 + i]))
         stores[-1].start()
 
-    for _, c in to_plane:
-        c.wait_recv()
-    mine = jnp.sum(red_xy[...], axis=0)
-    one_z[...] = mine
-    red_z[z] = mine
-
-    def rz(zz, slot):
-        return remote(one_z, red_z.at[slot], rz_ss.at[zz], rz_rs.at[slot], z_peer(zz))
-
-    for away in (4, 3, 5, 2, 6, 1, 7):
-        rz((z + away) % ZN, z).start()
     for j in range(1, ZN):
         rz((z + j) % ZN, (z + j) % ZN).wait_recv()
     mine = jnp.sum(red_z[...], axis=0)
@@ -596,8 +601,8 @@
 
     for c in stores:
         c.wait()
-    for c in halos:
-        c.wait_send()
+    halo.wait_send()
+    back.wait_send()
 
     def left(j, _):
         zz = (z + j) % ZN
@@ -715,12 +720,10 @@
             pltpu.VMEM((T + 8, thin), F32),
             pltpu.VMEM((T + 8, thin), F32),
             pltpu.VMEM((HEADS, 8, HD), F32),
-            pltpu.VMEM((16, thin), BF16),
-            pltpu.VMEM((16, thin), BF16),
-            pltpu.VMEM((16, wide), BF16),
-            pltpu.VMEM((8, thin), F32),
-            pltpu.VMEM((8, thin), F32),
-            pltpu.VMEM((HEADS, 8, HD), F32),
+            pltpu.VMEM((24, HD), F32),
+            pltpu.VMEM((24, HD), F32),
+            pltpu.VMEM((24, HD), F32),
+            pltpu.VMEM((24, HD), F32),
         ]
         for _ in range(2):
             scratch += [
@@ -743,7 +746,7 @@
             pltpu.SemaphoreType.DMA((9,)),
         ]
         dma = pltpu.SemaphoreType.DMA
-        for counts in ((3,), (3,), (2, 2, ZN), (2, 2, n_y), (2, 2, ZN), (1,), (n_dp // 2 * n_y,), (ZN,), (1,)):
+        for counts in ((1,), (1,), (2, 2, ZN), (2, 2, n_y), (2, 2, ZN), (1,), (n_dp // 2 * n_y,), (ZN,), (1,)):
             scratch += [dma(counts), dma(counts)]
         outs = pl.pallas_call(
             functools.partial(kernel, n_dp, n_ctx),

time: 71.2 us -> 70.6 us (level)
  no operation moved by 1% of the time
where the time goes in v5:
time: 70.6 us; the launch traced here: 70.4 us
  Pallas kernels  69.8 us (99%)
    pallas_call x1, Pallas kernels, shards(): pl.pallas_call(functools.partial(kernel, n_dp, n_ctx), out_shape=(jax.Sha...  67.6 us
    pallas_call x1, Pallas kernels, shards(): pl.pallas_call(writer, out_shape=(jax.ShapeDtypeStruct((T, wide), BF16),...  2.18 us

profile of v5, /device:TPU:1, one launch (start us, length us, event | category | flops | bytes accessed | tf_op | source)
XLA Modules:
  0.0 70.4 jit_solution(12587357591678451990)
XLA Ops:
  0.6 67.6 %shard_map.152 = (bf16[256,1024]{1,0:T(8,128)(2,1)}, bf16[256,128]{1,0:T(8,128)(2,1)}, bf16[256,128]{1,0:T(8,128)(2,1)}, bf16[256,1024]{1,0:T(8,128)(2,1)}, f32[2,24,128]{2,1,0:T(8,128)}) custom-call(s32[1,8]{1,0:T(1,128)} %lens_hbm.1, bf16[256,128]{1,0:T(8,128)(2,1)} %bitcast.12, bf16[256,128]{1,0:T(8,128)(2,1)} %bitcast.13, bf16[256,1024]{1,0:T(8,128)(2,1)} %bitcast.10, ...), custom_call_target="tpu_custom_call" | custom-call | tf_op jit(solution)/shard_map/pallas_call | solution.py:751
  68.2 2.2 %shard_map.153 = (bf16[256,1024]{1,0:T(8,128)(2,1)}, bf16[256,128]{1,0:T(8,128)(2,1)}, bf16[256,128]{1,0:T(8,128)(2,1)}, bf16[256,1024]{1,0:T(8,128)(2,1)}, f32[...) custom-call(bf16[256,1024]{1,0:T(8,128)(2,1)} %get-tuple-element.21.refs_0_, ...), custom_call_target="tpu_custom_call" | custom-call | tf_op jit(solution)/shard_map/pallas_call | solution.py:767

commit v6 on v5

--- a/solution.py
+++ b/solution.py
@@ -362,10 +362,11 @@
 
     for g in range(2):
 
+        for p in range(GROUP):
+            tail_head(GROUP * g + p)
+
         def tail_step(i, _, g=g):
-            p = (z // 2 + 2 + i) % GROUP
-            tail_head(GROUP * g + p)
-            send_tail(tail1, got1, 0, g, p)
+            send_tail(tail1, got1, 0, g, (z // 2 + 2 + i) % GROUP)
             return 0
 
         lax.fori_loop(0, GROUP, tail_step, 0)
@@ -484,6 +485,13 @@
 
     scan(tail2, got2, tot2, ytot2, send2, outg, 1, True)
 
+    def wait_states(send, take, phase, g):
+        def one(j, _):
+            b_arrival(send, take, phase, g, (z + j) % ZN).wait_recv()
+            return 0
+
+        lax.fori_loop(1, ZN, one, 0)
+
     def taps(g, x):
         return [jnp.sum(g * x[8 - j : 8 - j + T], axis=0, keepdims=True) for j in range(3)]
 
@@ -500,14 +508,9 @@
             )
 
     for g in range(2):
-
-        def last_step(i, _, g=g):
-            p = (z // 2 + 1 + i) % GROUP
-            wait_state(send2, outg, 1, g, p)
+        wait_states(send2, outg, 1, g)
+        for p in range(GROUP):
             last_head(GROUP * g + p)
-            return 0
-
-        lax.fori_loop(0, GROUP, last_step, 0)
     gq = gqt[...].T
     gk = gkt[...].T
     gqs[0:T, :] = gq

time: 70.6 us -> 70 us (level)
  no operation moved by 1% of the time
where the time goes in v6:
time: 70 us; the launch traced here: 69.9 us
  Pallas kernels  69.2 us (99%)
    pallas_call x1, Pallas kernels, shards(): pl.pallas_call(functools.partial(kernel, n_dp, n_ctx), out_shape=(jax.Sha...  67 us
    pallas_call x1, Pallas kernels, shards(): pl.pallas_call(writer, out_shape=(jax.ShapeDtypeStruct((T, wide), BF16),...  2.18 us

profile of v6, /device:TPU:1, one launch (start us, length us, event | category | flops | bytes accessed | tf_op | source)
XLA Modules:
  0.0 69.9 jit_solution(15077859007611326065)
XLA Ops:
  0.6 67.0 %shard_map.152 = (bf16[256,1024]{1,0:T(8,128)(2,1)}, bf16[256,128]{1,0:T(8,128)(2,1)}, bf16[256,128]{1,0:T(8,128)(2,1)}, bf16[256,1024]{1,0:T(8,128)(2,1)}, f32[2,24,128]{2,1,0:T(8,128)}) custom-call(s32[1,8]{1,0:T(1,128)} %lens_hbm.1, bf16[256,128]{1,0:T(8,128)(2,1)} %bitcast.12, bf16[256,128]{1,0:T(8,128)(2,1)} %bitcast.13, bf16[256,1024]{1,0:T(8,128)(2,1)} %bitcast.10, ...), custom_call_target="tpu_custom_call" | custom-call | tf_op jit(solution)/shard_map/pallas_call | solution.py:754
  67.7 2.2 %shard_map.153 = (bf16[256,1024]{1,0:T(8,128)(2,1)}, bf16[256,128]{1,0:T(8,128)(2,1)}, bf16[256,128]{1,0:T(8,128)(2,1)}, bf16[256,1024]{1,0:T(8,128)(2,1)}, f32[...) custom-call(bf16[256,1024]{1,0:T(8,128)(2,1)} %get-tuple-element.21.refs_0_, ...), custom_call_target="tpu_custom_call" | custom-call | tf_op jit(solution)/shard_map/pallas_call | solution.py:770

commit v7 on v6

--- a/solution.py
+++ b/solution.py
@@ -165,7 +165,8 @@
         return {"ctx": yy * ZN + z}
 
     barrier = pltpu.get_barrier_semaphore()
-    greeted = [z_peer((z + j) % ZN) for j in range(1, ZN)]
+    greeted = [z_peer((z + j) % ZN) for j in (4, 3, 5)] + [{"ctx": after}, {"ctx": before}]
+    greeted += [z_peer((z + j) % ZN) for j in (2, 6, 1, 7)]
     other = {"dp": dp + 1 - 2 * core}
     plane = []
     for j in range(1, n_x * n_y):
@@ -173,7 +174,7 @@
         yy = (y + j % n_y) % n_y
         plane.append((xx * n_y + yy, {"dp": xx * 2 + core, "ctx": yy * ZN + z}))
     greeted += [peer for _, peer in plane]
-    greeted += [other, {"ctx": after}, {"ctx": before}]
+    greeted += [other]
     for peer in greeted:
         pl.semaphore_signal(barrier, inc=1, device_id=peer, device_id_type=MESH)
 

time: 70 us -> 69.6 us (level)
  no operation moved by 1% of the time
where the time goes in v7:
time: 69.6 us; the launch traced here: 69.5 us
  Pallas kernels  68.9 us (99%)
    pallas_call x1, Pallas kernels, shards(): pl.pallas_call(functools.partial(kernel, n_dp, n_ctx), out_shape=(jax.Sha...  66.7 us
    pallas_call x1, Pallas kernels, shards(): pl.pallas_call(writer, out_shape=(jax.ShapeDtypeStruct((T, wide), BF16),...  2.18 us

profile of v7, /device:TPU:1, one launch (start us, length us, event | category | flops | bytes accessed | tf_op | source)
XLA Modules:
  0.0 69.5 jit_solution(14696386711851460823)
XLA Ops:
  0.6 66.7 %shard_map.152 = (bf16[256,1024]{1,0:T(8,128)(2,1)}, bf16[256,128]{1,0:T(8,128)(2,1)}, bf16[256,128]{1,0:T(8,128)(2,1)}, bf16[256,1024]{1,0:T(8,128)(2,1)}, f32[2,24,128]{2,1,0:T(8,128)}) custom-call(s32[1,8]{1,0:T(1,128)} %lens_hbm.1, bf16[256,128]{1,0:T(8,128)(2,1)} %bitcast.12, bf16[256,128]{1,0:T(8,128)(2,1)} %bitcast.13, bf16[256,1024]{1,0:T(8,128)(2,1)} %bitcast.10, ...), custom_call_target="tpu_custom_call" | custom-call | tf_op jit(solution)/shard_map/pallas_call | solution.py:755
  67.3 2.2 %shard_map.153 = (bf16[256,1024]{1,0:T(8,128)(2,1)}, bf16[256,128]{1,0:T(8,128)(2,1)}, bf16[256,128]{1,0:T(8,128)(2,1)}, bf16[256,1024]{1,0:T(8,128)(2,1)}, f32[...) custom-call(bf16[256,1024]{1,0:T(8,128)(2,1)} %get-tuple-element.21.refs_0_, ...), custom_call_target="tpu_custom_call" | custom-call | tf_op jit(solution)/shard_map/pallas_call | solution.py:771
